TPU v7x, 1024 devices: a whole 8x8x8 slice. The times are simulated.
1024 devices in a mesh: dp: 4 (over z_hi, core), ctx: 32 (over x, z_lo), tensor: 8 (over y).
Axes of the slice: x: 8, y: 8, z: 8 (z_hi: 2, z_lo: 4; z = z_hi * 4 + z_lo), core: 2. Of those that a mesh axis runs over, the one named last changes fastest.
Arguments:
- out_grad: bfloat16 [4, 8192, 4096], P('dp', ('ctx', 'tensor')), may hold values from -1 to 1
- prev_state: bfloat16 [4, 8192, 4096], P('dp', 'ctx', 'tensor'), may hold values from -6 to 6
- boundary: int32 [4, 8192], P('dp', 'ctx'), may hold values 0 or 1
- angle_code: int32 [64, 32], P('tensor'), may hold values from 0 to 4095
- radius_code: int32 [64, 32], P('tensor'), may hold values from 0 to 1023
- reflect: float32 [64, 4, 64], P('tensor'), may hold values from -6 to 6
Outputs:
- grad_input: bfloat16 [4, 8192, 4096], P('dp', 'ctx', 'tensor')
- grad_transition: float32 [64, 64, 64], P('tensor')
All inputs are finite; a program needn't handle non-finite values. No bound on the sum of `boundary` on one device may be relied on, other than what follows from the above.
Results may differ from a plain program's by a relative error of at most 0.003.
Values may be sent and summed in bfloat16 or wider, within the bound.
A program may use at most 64 MiB of HBM per device.

v0:
```python
import math

import jax
import jax.numpy as jnp
from jax import lax
from jax.sharding import Mesh
from jax.sharding import PartitionSpec as P

SUBLEN = 16
CTX = ("ctx_0", "ctx_1")
DP_CTX = ("dp", "ctx_0", "ctx_1")
CTX_TENSOR = ("ctx_0", "ctx_1", "tensor")


def neutral_like(array, identity):
    return jax.tree.map(
        lambda a, e: jnp.broadcast_to(jnp.asarray(e, a.dtype), a.shape), array, identity
    )


def carried_in(array, axes, combine, identity):
    before = start = neutral_like(array, identity)
    so_far = array
    for axis in reversed(axes):
        peers, position = (lax.axis_size(axis), lax.axis_index(axis))
        pieces = jax.tree.map(lambda part: lax.all_gather(part, axis), so_far)
        inside, so_far = (start, start)
        for k in reversed(range(peers)):
            passed = k > position
            so_far = combine(so_far, jax.tree.map(lambda part: part[k], pieces))
            inside = jax.tree.map(lambda new, old: jnp.where(passed, new, old), so_far, inside)
        before = combine(inside, before)
    return before


def transition(angle_code, radius_code, reflect):
    block_count = radius_code.shape[0]
    block_size = 2 * radius_code.shape[1]
    rates = jnp.exp2(-(4.0 + radius_code.astype(jnp.float32) * (10.0 / 1024.0)))
    radius = 1.0 - rates
    angles = angle_code.astype(jnp.float32) * (math.pi / 4096.0)
    cosine = jnp.repeat(radius * jnp.cos(angles), 2, axis=1)[:, :, None]
    sine_part = jnp.repeat(radius * jnp.sin(angles), 2, axis=1)[:, :, None]
    row_index = jnp.arange(block_size)[:, None]
    col_index = jnp.arange(block_size)[None, :]
    on_diagonal = row_index == col_index
    upper_pair = (row_index % 2 == 0) & (col_index == row_index + 1)
    lower_pair = (row_index % 2 == 1) & (col_index == row_index - 1)
    zero_value = jnp.float32(0.0)
    rotation = (
        jnp.where(on_diagonal[None], cosine, zero_value)
        + jnp.where(upper_pair[None], -sine_part, zero_value)
        + jnp.where(lower_pair[None], sine_part, zero_value)
    )
    basis_now = jnp.broadcast_to(
        jnp.eye(block_size, dtype=jnp.float32), (block_count, block_size, block_size)
    )
    for reflect_index in range(4):
        reflector = reflect[:, reflect_index, :]
        norm_sq = jnp.sum(reflector * reflector, axis=1)
        projected = jnp.einsum("bij,bj->bi", basis_now, reflector, precision=lax.Precision.HIGHEST)
        basis_now = (
            basis_now - 2.0 * projected[:, :, None] * reflector[:, None, :] / norm_sq[:, None, None]
        )
    rotated = jnp.einsum("bij,bjk->bik", basis_now, rotation, precision=lax.Precision.HIGHEST)
    return jnp.einsum("bik,blk->bil", rotated, basis_now, precision=lax.Precision.HIGHEST)


def apply_blocks(matrix, vectors):
    return jnp.einsum("bxy,...by->...bx", matrix, vectors, precision=lax.Precision.HIGHEST)


def matrix_blocks(left_side, right_side):
    return jnp.einsum("bxy,byz->bxz", left_side, right_side, precision=lax.Precision.HIGHEST)


def power_stack(matrix, how_many):
    block_count, block_size = (matrix.shape[0], matrix.shape[1])
    stacked = jnp.broadcast_to(
        jnp.eye(block_size, dtype=jnp.float32), (1, block_count, block_size, block_size)
    )
    current = matrix
    while stacked.shape[0] < how_many:
        extended = jnp.einsum("qbxy,byz->qbxz", stacked, current, precision=lax.Precision.HIGHEST)
        stacked = jnp.concatenate([stacked, extended], axis=0)
        current = matrix_blocks(current, current)
    return stacked[:how_many]


def matrix_power(matrix, exponent_count):
    result = None
    base = matrix
    remaining = exponent_count
    while remaining > 0:
        if remaining % 2 == 1:
            result = base
        remaining = remaining // 2
        if remaining > 0:
            base = matrix_blocks(base, base)
    return result


def body(out_grad, prev_state, boundary, angle_code, radius_code, reflect):
    local_grad = lax.all_to_all(out_grad, "tensor", split_axis=2, concat_axis=1, tiled=True)
    transit = transition(angle_code, radius_code, reflect)
    transposed = jnp.swapaxes(transit, 1, 2)
    block_count, block_size = (transit.shape[0], transit.shape[1])
    token_count = local_grad.shape[1]
    sub_count = token_count // SUBLEN
    grad_rows = (
        local_grad[0].astype(jnp.float32).reshape(sub_count, SUBLEN, block_count, block_size)
    )
    retain = jnp.where(boundary[0] == 1, jnp.float32(0.6), jnp.float32(1.0)).reshape(
        sub_count, SUBLEN
    )

    def backstep(state_next, inputs):
        grad_row, keep_row = inputs
        adjoint = grad_row + keep_row[:, None, None] * apply_blocks(transposed, state_next)
        return (adjoint, adjoint)

    zero_state = jnp.zeros((sub_count, block_count, block_size), jnp.float32)
    unused_state, local_adj = lax.scan(
        backstep,
        zero_state,
        (jnp.swapaxes(grad_rows, 0, 1), jnp.swapaxes(retain, 0, 1)),
        reverse=True,
    )
    log_keep = jnp.log(retain)
    tail_logs = jnp.flip(jnp.cumsum(jnp.flip(log_keep, 1), axis=1), 1)
    tail_scale = jnp.exp(tail_logs)
    sub_logs = tail_logs[:, 0]
    total_log = jnp.sum(sub_logs)
    small_powers = power_stack(transposed, SUBLEN + 1)
    block_power = small_powers[SUBLEN]
    device_power = matrix_power(block_power, sub_count)
    starts = local_adj[0]

    def entry_step(entry_now, inputs):
        start_row, sub_log = inputs
        entry_before = start_row + jnp.exp(sub_log) * apply_blocks(block_power, entry_now)
        return (entry_before, entry_now)

    zero_vector = jnp.zeros((block_count, block_size), jnp.float32)
    device_first, unused_entries = lax.scan(
        entry_step, zero_vector, (starts, sub_logs), reverse=True
    )
    device_map = jnp.exp(total_log) * device_power

    def compose(earlier, nearer):
        return (
            nearer[0] + apply_blocks(nearer[1], earlier[0]),
            matrix_blocks(nearer[1], earlier[1]),
        )

    identity_blocks = jnp.broadcast_to(
        jnp.eye(block_size, dtype=jnp.float32), (block_count, block_size, block_size)
    )
    incoming, unused_matrix = carried_in(
        (device_first, device_map), CTX, compose, (zero_vector, identity_blocks)
    )
    unused_first, entry_full = lax.scan(entry_step, incoming, (starts, sub_logs), reverse=True)
    small_chosen = jnp.flip(small_powers[1:], 0)
    correction = jnp.einsum(
        "ibxy,jby->ijbx", small_chosen, entry_full, precision=lax.Precision.HIGHEST
    )
    adjoint_all = local_adj + jnp.swapaxes(tail_scale, 0, 1)[:, :, None, None] * correction
    grad_input = (
        jnp.swapaxes(adjoint_all, 0, 1)
        .reshape(1, token_count, block_count * block_size)
        .astype(jnp.bfloat16)
    )
    previous = jnp.swapaxes(
        prev_state[0].astype(jnp.float32).reshape(sub_count, SUBLEN, block_count, block_size), 0, 1
    )
    partial_grad = jnp.einsum(
        "ijbx,ijby->bxy", adjoint_all, previous, precision=lax.Precision.HIGHEST
    )
    summed = lax.psum(partial_grad, DP_CTX)
    return (grad_input, summed)


def solution(mesh):
    split = Mesh(
        mesh.devices.reshape(mesh.shape["dp"], 8, 4, mesh.shape["tensor"]),
        ("dp", "ctx_0", "ctx_1", "tensor"),
    )
    in_specs = (
        P("dp", CTX_TENSOR, None),
        P("dp", CTX, "tensor"),
        P("dp", CTX),
        P("tensor", None),
        P("tensor", None),
        P("tensor", None, None),
    )
    out_specs = (P("dp", CTX, "tensor"), P("tensor", None, None))
    return jax.shard_map(body, mesh=split, in_specs=in_specs, out_specs=out_specs, check_vma=False)
```

profile of v0, /device:TPU:1, one launch (start us, length us, event | category | flops | bytes accessed | tf_op | source)
XLA Modules:
  0.0 485.3 jit_solution(3568121636967321546)
XLA Ops:
  21.7 2.0 bitcast_dynamic-update-slice_fusion.3
  23.8 4.2 constant_dynamic-update-slice_fusion.3
  28.0 2.0 copy-done
  30.6 1.8 copy-done.2
  35.3 23.1 %all-gather.1 = f32[32,64,64]{2,1,0:T(8,128)S(1)} all-gather(f32[8,64,64]{2,1,0:T(8,128)S(1)} %convolution_multiply_fusion.1), channel_id=3, replica_groups=mesh['dp'=4,'ctx_0'=8,'ctx_1'=4,'tensor'=8] {'ctx_1'}, dimensions={0}, use_global_device_ids=true | all-gather | bytes 655360 | tf_op jit(solution)/shard_map/all_gather | solution.py:26
  60.7 3.8 copy.70
  65.0 23.4 %reduce.7 = bf16[4096,32]{1,0:T(8,128)(2,1)S(1)} reduce(bf16[4096,1,32]{2,1,0:T(2,128)(2,1)} %bitcast.303, bf16[]{:T(256)} %broadcast.167), dimensions={1}, to_apply=%bitcast.203.reduce_sub_computation | reduce | bytes 524290
  88.5 1.7 reshape.278
  90.1 10.3 %all-to-all-start = ((bf16[8,2,8192]{2,1,0:T(2,128)(2,1)}), bf16[8,2,8192]{2,1,0:T(2,128)(2,1)S(1)}, u32[]{:S(2)}, u32[]{:S(2)}) async-start(bf16[8,2,8192]{2,1,0:T(2,128)(2,1)} %reshape.278), calls=%async_computation | async-start | bytes 524288 | tf_op jit(solution)/shard_map/all_to_all | solution.py:104
  102.2 2.1 reshape.170
  104.8 2.0 fusion.37
  106.8 3.0 all-to-all-done
  109.8 3.7 reshape.279
  113.5 4.8 bitcast_convert_fusion
  118.3 2.2 copy.71
  121.8 22.7 %while.49 = (s32[]{:T(128)}, f32[16,8,64]{2,0,1:T(8,128)S(1)}, f32[16,16,8,64]{3,1,2,0:T(8,128)S(1)}, f32[16,16,8,64]{3,2,0,1:T(8,128)}, f32[16,16]{1,0:T(8,128)...) while((s32[]{:T(128)}, f32[16,8,64]{2,0,1:T(8,128)S(1)}, ...), condition=%wide.region_5.6_spmd.clone, body=%wide.region_4.5_spmd.clone.sunk | while | flops 6316036 | bytes 656127 | solution.py:123
  145.0 29.3 %while.50 = (s32[]{:T(128)}, f32[8,64]{1,0:T(8,128)S(1)}, f32[16,8,64]{2,1,0:T(8,128)S(1)}, f32[16]{0:T(128)S(1)}, f32[8,64,64]{2,1,0:T(8,128)S(1)}, /*index=5*/s32[]{:T(128)}, s32[]{:T(128)}, s32[]{:T(128)}) while((s32[]{:T(128)}, f32[8,64]{1,0:T(8,128)S(1)}, f32[16,8,64]{2,1,0:T(8,128)S(1)}, f32[16]{0:T(128)S(1)}, ...), condition=%wide.region_8.9_spmd.clone, body=%wide.region_7.8_spmd.clone.sunk | while | flops 394756 | bytes 145543 | solution.py:145
  174.2 10.5 %all-gather = f32[32,64]{1,0:T(8,128)S(1)} all-gather(f32[8,64]{1,0:T(8,128)S(1)} %get-tuple-element.350), channel_id=2, replica_groups=mesh['dp'=4,'ctx_0'=8,'ctx_1'=4,'tensor'=8] {'ctx_1'}, dimensions={0}, use_global_device_ids=true | all-gather | bytes 10240 | tf_op jit(solution)/shard_map/all_gather | solution.py:26
  186.4 20.9 %all-gather.2 = f32[64,64]{1,0:T(8,128)} all-gather(f32[8,64]{1,0:T(8,128)S(1)} %get-tuple-element.479), channel_id=4, replica_groups=mesh['dp'=4,'ctx_0'=8,'ctx_1'=4,'tensor'=8] {'ctx_0'}, dimensions={0}, use_global_device_ids=true | all-gather | bytes 18432 | tf_op jit(solution)/shard_map/all_gather | solution.py:26
  207.8 1.5 fusion.110
  210.0 1.5 fusion.111
  212.1 1.5 fusion.112
  214.3 1.5 fusion.113
  216.4 1.5 fusion.114
  218.6 1.5 fusion.115
  220.7 1.5 fusion.116
  222.9 1.5 fusion.117
  225.6 29.2 %while.48 = (s32[]{:T(128)}, f32[8,64]{1,0:T(8,128)S(1)}, f32[16,8,64]{2,1,0:T(8,128)S(1)}, f32[16,8,64]{2,1,0:T(8,128)S(1)}, f32[16]{0:T(128)S(1)}, /*index=5*/f32[8,64,64]{2,1,0:T(8,128)S(1)}, s32[]{:T(128)}, s32[]{:T(128)}) while((s32[]{:T(128)}, f32[8,64]{1,0:T(8,128)S(1)}, f32[16,8,64]{2,1,0:T(8,128)S(1)}, ...), condition=%wide.region_11.12_spmd, body=%wide.region_10.11_spmd.sunk | while | flops 394243 | bytes 149633 | solution.py:162
  254.8 3.9 fusion.23
  258.7 2.3 convolution_bitcast_fusion.4
  262.5 214.4 %all-reduce.2.cloned.1.call-done = f32[8,64,64]{2,1,0:T(8,128)} async-done(((f32[8,64,64]{2,1,0:T(8,128)}), f32[8,64,64]{2,1,0:T(8,128)}) %all-reduce.2.cloned.1.call-update) | async-done | bytes 131088 | tf_op jit(solution)/shard_map/psum | solution.py:179
  476.8 1.7 copy.226
  (308 shorter events, 91.3 us)
Async XLA Ops:
  7.2 7.0 %copy-start.8 = (f32[8,4,64]{2,1,0:T(4,128)S(1)}, f32[8,4,64]{2,1,0:T(4,128)}, u32[]{:S(2)}) copy-start(f32[8,4,64]{2,1,0:T(4,128)} %param.17) | copy-start | bytes 24580
  7.2 200.6 %all-gather.6.cloned.1.call-start = ((), (), s32[]{:S(2)}) async-start(), calls=%async_computation.2 | async-start | bytes 2359296 | tf_op jit(solution)/shard_map/all_gather | solution.py:26
  15.5 2.4 copy-start.1
  23.8 9.4 %copy-start.9 = (s32[1,256]{1,0:T(1,128)S(1)}, s32[1,256]{1,0:T(1,128)}, u32[]{:S(2)}) copy-start(s32[1,256]{1,0:T(1,128)} %param.14) | copy-start | bytes 3076
  28.0 2.0 copy-start
  28.0 4.4 copy-start.2
  32.7 27.9 %copy-start.7 = (bf16[1,32,4096]{2,1,0:T(8,128)(2,1)S(1)}, bf16[1,32,4096]{2,1,0:T(8,128)(2,1)}, u32[]{:S(2)}) copy-start(bf16[1,32,4096]{2,1,0:T(8,128)(2,1)} %param.12) | copy-start | bytes 786436
  58.8 29.7 %copy-start.4 = (f32[8,64,64]{2,1,0:T(8,128)}, f32[8,64,64]{2,1,0:T(8,128)S(1)}, u32[]{:S(2)}) copy-start(f32[8,64,64]{2,1,0:T(8,128)S(1)} %fusion.57) | copy-start | bytes 393220
  64.5 40.3 %copy-start.3 = (f32[8,64,64]{2,1,0:T(8,128)S(1)}, f32[8,64,64]{2,1,0:T(8,128)}, u32[]{:S(2)}) copy-start(f32[8,64,64]{2,1,0:T(8,128)} %fusion.109) | copy-start | bytes 393220
  90.1 19.7 %all-to-all-start = ((bf16[8,2,8192]{2,1,0:T(2,128)(2,1)}), bf16[8,2,8192]{2,1,0:T(2,128)(2,1)S(1)}, u32[]{:S(2)}, u32[]{:S(2)}) async-start(bf16[8,2,8192]{2,1,0:T(2,128)(2,1)} %reshape.278), calls=%async_computation | async-start | bytes 524288 | tf_op jit(solution)/shard_map/all_to_all | solution.py:104
  100.4 376.4 %all-reduce.2.cloned.1.call-start = ((), (), s32[]{:S(2)}) async-start(), calls=%async_computation.1 | async-start | bytes 524288 | tf_op jit(solution)/shard_map/psum | solution.py:179
  184.8 40.3 %copy-start.5 = (f32[8,64,64]{2,1,0:T(8,128)S(1)}, f32[8,64,64]{2,1,0:T(8,128)}, u32[]{:S(2)}) copy-start(f32[8,64,64]{2,1,0:T(8,128)} %fusion.37) | copy-start | bytes 393220
  225.1 33.6 %copy-start.6 = (bf16[16,16,8,64]{3,2,1,0:T(8,128)(2,1)S(1)}, bf16[16,16,8,64]{3,2,1,0:T(8,128)(2,1)}, u32[]{:S(2)}) copy-start(bf16[16,16,8,64]{3,2,1,0:T(8,128)(2,1)} %reshape.170) | copy-start | bytes 786436
Sparse Core Ops, SparseCore 0:
  60.8 53.9 all-gather.5
  261.1 215.6 all-reduce.1
where the time goes:
time: 489 us; the launch traced here: 485 us
  waiting for transfers between devices  217 us (44%)
  matrix products  68.7 us (14%)
  local copies, waits for them, and re-layouts  59 us (12%)
  blocking collectives  54.5 us (11%)
  other arithmetic  36.4 us (7%)
  loops' own time  23.4 us (5%)
  between operations  15.2 us (3%)
  starting transfers between devices  10.6 us (2%)
    psum x1, waiting for transfers between devices, body(): summed = lax.psum(partial_grad, DP_CTX)  214 us
    all_gather x3, blocking collectives, carried_in(): pieces = jax.tree.map(lambda part: lax.all_gather(part, axis), so_far)  54.5 us
    dot_general x62, matrix products, apply_blocks(): jnp.einsum('bxy,...by->...bx', matrix, vectors, precision=lax.Precision.H...  39.6 us
    unnamed x3, other arithmetic  23.5 us
    dynamic_slice x32, local copies, waits for them, and re-layouts, body(): lax.scan(entry_step, zero_vector, (starts, sub_logs), reverse=True)  18.9 us
    unnamed x29, local copies, waits for them, and re-layouts  16.2 us
    dynamic_slice x16, local copies, waits for them, and re-layouts, body(): lax.scan(backstep, zero_state, (jnp.swapaxes(grad_rows, 0, 1), jnp.swapax...  13.6 us
    another operation x1, loops' own time, body(): lax.scan(entry_step, zero_vector, (starts, sub_logs), reverse=True)  11.4 us
  transfers between devices with their start and end apart: 3, of which 2 were waited for; matrix products, arithmetic and copies ran while one was open for 19% of the time, Pallas kernels for 0%

commit v1 on v0

v1 whole, which is shorter than its diff:
```python
import functools
import math

import jax
import jax.numpy as jnp
from jax import lax
from jax.experimental import pallas as pl
from jax.experimental.pallas import tpu as pltpu
from jax.sharding import Mesh
from jax.sharding import PartitionSpec as P

F32, BF16, I32 = jnp.float32, jnp.bfloat16, jnp.int32
NN = (((1,), (0,)), ((), ()))
NT = (((1,), (1,)), ((), ()))
TN = (((0,), (0,)), ((), ()))
MESH = pl.DeviceIdType.MESH

TOK, CH, SUB, STEP = 256, 512, 8, 32
BS, NB = 64, 8
DP = ("zh", "core")
CTX = ("x", "zl")


def iota(shape, axis):
    return lax.broadcasted_iota(I32, shape, axis)


def dot(a, b, dims):
    return lax.dot_general(a, b, dims, preferred_element_type=F32)


def fdot(a, b, dims):
    return lax.dot_general(a, b, dims, precision=lax.Precision.HIGHEST, preferred_element_type=F32)


def split(a):
    hi = a.astype(BF16)
    return hi, (a - hi.astype(F32)).astype(BF16)


def cmul(a, b):
    return a[0] * b[0] - a[1] * b[1], a[0] * b[1] + a[1] * b[0]


def cadd(a, b):
    return a[0] + b[0], a[1] + b[1]


def cwhere(m, a, b):
    return jnp.where(m, a[0], b[0]), jnp.where(m, a[1], b[1])


def compact(full):
    lane_block = (iota((BS, 256), 1) % 128) // 32
    out = jnp.zeros((BS, 256), F32)
    for bb in range(4):
        out = jnp.where(lane_block == bb, full[BS * bb : BS * bb + BS], out)
    return out


def kernel(
    sizes, og, ps, bd, ac, rc, rf, gi, gt,
    g, pv, whi, wlo, kl, wq, un, cn, qc, gc, gr, bz, bx, gsum, rcore, rx, rz,
    lsem, ysend, yrecv, bzs, bzr, bxs, bxr, css, csr, xss, xsr, zss, zsr, xas, xar, cas, car,
):
    n_zh, n_core, n_x, n_zl, n_y = sizes
    n_z = n_zh * n_zl
    zh, core, x, zl, y = (lax.axis_index(a) for a in ("zh", "core", "x", "zl", "y"))
    z = zh * n_zl + zl
    rows = TOK // n_y

    def at_y(d):
        return {"y": lax.rem(y + d, n_y)}

    def at_x(d):
        return {"x": lax.rem(x + d, n_x)}

    def at_z(d):
        k = lax.rem(z + d, n_z)
        return {"zh": k // n_zl, "zl": lax.rem(k, n_zl)}

    def at_zl(d):
        return {"zl": lax.rem(zl + d, n_zl)}

    sibling = {"core": 1 - core}
    partners = (
        [at_y(d) for d in range(1, n_y)]
        + [at_x(d) for d in range(1, n_x)]
        + [at_z(d) for d in range(1, n_z)]
        + [sibling]
    )
    barrier = pltpu.get_barrier_semaphore()
    for partner in partners:
        pl.semaphore_signal(barrier, inc=1, device_id=partner, device_id_type=MESH)

    def remote(src, dst, send, recv, where):
        return pltpu.make_async_remote_copy(
            src_ref=src, dst_ref=dst, send_sem=send, recv_sem=recv, device_id=where, device_id_type=MESH
        )

    load_prev = pltpu.make_async_copy(ps.at[0], pv, lsem.at[0])
    load_prev.start()
    own_rows = pl.ds(pl.multiple_of(y * rows, rows), rows)
    load_own = pltpu.make_async_copy(
        og.at[0, :, pl.ds(pl.multiple_of(y * CH, CH), CH)], g.at[own_rows], lsem.at[1]
    )
    load_own.start()
    pl.semaphore_wait(barrier, len(partners))

    a2a = []
    for d in range(1, n_y):
        k = lax.rem(y + d, n_y)
        a2a.append(
            remote(
                og.at[0, :, pl.ds(pl.multiple_of(k * CH, CH), CH)],
                g.at[own_rows], ysend.at[d], yrecv.at[d], {"y": k},
            )
        )
        a2a[-1].start()

    pick = (iota((32, 128), 1) % 32 == iota((32, 128), 0)).astype(F32)
    acode = fdot(ac[...].astype(F32), pick, NN)
    rcode = fdot(rc[...].astype(F32), pick, NN)
    radius = 1.0 - jnp.exp2(-(4.0 + rcode * (10.0 / 1024.0)))
    angle = acode * (math.pi / 4096.0)
    lam_r, lam_i = radius * jnp.cos(angle), -radius * jnp.sin(angle)
    lam = []
    for h in range(2):
        mine = iota((NB, 128), 0) == 4 * h + iota((NB, 128), 1) // 32
        lam.append(
            tuple(
                jnp.broadcast_to(jnp.sum(jnp.where(mine, v, 0.0), axis=0, keepdims=True), (SUB, 128))
                for v in (lam_r, lam_i)
            )
        )

    r_id, t_id = iota((TOK, TOK), 0), iota((TOK, TOK), 1)
    chosen = t_id == (r_id % SUB) * STEP + r_id // SUB
    marks = jnp.where(chosen & (bd[...] == 1), 1.0, 0.0).astype(BF16)
    keep = jnp.where(dot(marks, jnp.ones((TOK, 128), BF16), NN) > 0.5, F32(0.6), F32(1.0))
    for h in range(2):
        for part in range(2):
            kl[2 * h + part] = keep * lam[h][part][0:1]

    lane = iota((BS, 256), 1)
    spread = (iota((NB, 256), 1) // 32 == iota((NB, 256), 0)).astype(F32)
    xs = [(iota((BS, 256), 0) == 2 * (lane % 32) + part).astype(F32) for part in range(2)]
    for k in (3, 2, 1, 0):
        v = fdot(rf[:, k, :], spread, TN)
        scale = 2.0 / jnp.sum(v * v, axis=0, keepdims=True)
        xs = [m - v * (scale * jnp.sum(v * m, axis=0, keepdims=True)) for m in xs]
    lane_block = (lane % 128) // 32
    for h in range(2):
        half = jnp.concatenate([m[:, 128 * h : 128 * h + 128] for m in xs], axis=1)
        for bb in range(4):
            hi, lo = split(jnp.where(lane_block == bb, half, 0.0))
            whi[h, BS * bb : BS * bb + BS, :] = hi
            wlo[h, BS * bb : BS * bb + BS, :] = lo

    def at_q(ref, q):
        return [(ref[2 * h, pl.ds(q * SUB, SUB), :], ref[2 * h + 1, pl.ds(q * SUB, SUB), :]) for h in range(2)]

    def at_t(ref, q):
        return [
            (ref[2 * h, pl.ds(q, SUB, stride=STEP), :], ref[2 * h + 1, pl.ds(q, SUB, stride=STEP), :])
            for h in range(2)
        ]

    def put_t(ref, q, value):
        for h in range(2):
            for part in range(2):
                ref[2 * h + part, pl.ds(q, SUB, stride=STEP), :] = value[h][part]

    def weights(i, w):
        for u in range(4):
            q = STEP - 1 - (4 * i + u)
            w = [cmul(a, b) for a, b in zip(at_q(kl, q), w)]
            for h in range(2):
                for part in range(2):
                    wq[2 * h + part, pl.ds(q * SUB, SUB), :] = w[h][part]
        return w

    one = (jnp.ones((SUB, 128), F32), jnp.zeros((SUB, 128), F32))
    m1 = lax.fori_loop(0, STEP // 4, weights, [one, one])
    sub = iota((SUB, 128), 0)

    def later(v, m):
        return tuple(pltpu.roll(p, SUB - m, 0) for p in v)

    zero = (jnp.zeros((SUB, 128), F32), jnp.zeros((SUB, 128), F32))
    hops, base = [], []
    for h in range(2):
        steps = [cwhere(sub < SUB - 1, m1[h], zero)]
        b = cwhere(sub < SUB - 1, later(m1[h], 1), one)
        for m in (1, 2, 4):
            if m > 1:
                steps.append(cmul(steps[-1], later(steps[-1], m // 2)))
            b = cmul(b, cwhere(sub < SUB - m, later(b, m), one))
        hops.append(steps)
        base.append(b)

    def enter(i, _):
        for u in range(4):
            q = 4 * i + u
            put_t(un, q, [cmul(a, b) for a, b in zip(at_q(wq, q), base)])
        return 0

    lax.fori_loop(0, STEP // 4, enter, 0)
    mu = [(un[2 * h, 0:1, :], un[2 * h + 1, 0:1, :]) for h in range(2)]

    def with_prev(ref, h):
        prev = pv[:, 256 * h : 256 * h + 256]
        hi, lo = split(jnp.concatenate([ref[2 * h], ref[2 * h + 1]], axis=1))
        return compact(dot(prev, hi, TN) + dot(prev, lo, TN))

    load_prev.wait()
    for h in range(2):
        qc[:, 256 * h : 256 * h + 256] = with_prev(un, h)

    load_own.wait()
    for copy in a2a:
        copy.wait_recv()
    for h in range(2):
        rows_h = g[:, 256 * h : 256 * h + 256]
        turned = dot(rows_h, whi[h], NN) + dot(rows_h, wlo[h], NN)
        cn[2 * h] = turned[:, :128]
        cn[2 * h + 1] = turned[:, 128:]

    def back(i, c):
        for u in range(4):
            q = STEP - 1 - (4 * i + u)
            c = [cadd(a, cmul(b, v)) for a, b, v in zip(at_t(cn, q), at_q(kl, q), c)]
            put_t(cn, q, c)
        return c

    first = lax.fori_loop(0, STEP // 4, back, [zero, zero])
    entering = []
    for h in range(2):
        v = first[h]
        for m, step in zip((1, 2, 4), hops[h]):
            v = cadd(v, cmul(step, later(v, m)))
        entering.append(cwhere(sub < SUB - 1, later(v, 1), zero))
        for part in range(2):
            bz[zl, 2 * part + h : 2 * part + h + 1, :] = v[part][0:1]
            bz[zl, 4 + 2 * part + h : 5 + 2 * part + h, :] = mu[h][part]

    zcopies = [remote(bz.at[zl], bz.at[zl], bzs.at[d], bzr.at[d], at_zl(d)) for d in range(1, n_zl)]
    for copy in zcopies:
        copy.start()

    def fix(i, _):
        for u in range(4):
            q = 4 * i + u
            put_t(cn, q, [cadd(a, cmul(b, v)) for a, b, v in zip(at_t(cn, q), at_q(wq, q), entering)])
        return 0

    lax.fori_loop(0, STEP // 4, fix, 0)
    for copy in zcopies:
        copy.wait_recv()

    def firsts(ref, j):
        return ((ref[j, 0:2, :], ref[j, 2:4, :]), (ref[j, 4:6, :], ref[j, 6:8, :]))

    zero2 = (jnp.zeros((2, 128), F32), jnp.zeros((2, 128), F32))
    one2 = (jnp.ones((2, 128), F32), jnp.zeros((2, 128), F32))

    def chain(ref, count, me):
        inside, passing = zero2, one2
        total, span = zero2, one2
        for j in reversed(range(count)):
            f, m = firsts(ref, j)
            total, span = cadd(f, cmul(m, total)), cmul(m, span)
            inside = cwhere(j > me, total, inside)
            passing = cwhere(j > me, span, passing)
        return inside, passing, total, span

    inside, passing, total, span = chain(bz, n_zl, zl)
    for part in range(2):
        bx[x, 2 * part : 2 * part + 2, :] = total[part]
        bx[x, 4 + 2 * part : 6 + 2 * part, :] = span[part]
    xcopies = [remote(bx.at[x], bx.at[x], bxs.at[d], bxr.at[d], at_x(d)) for d in range(1, n_x)]
    for copy in xcopies:
        copy.start()
    for h in range(2):
        gc[:, 256 * h : 256 * h + 256] = with_prev(cn, h)
    for copy in xcopies:
        copy.wait_recv()
    beyond, _, _, _ = chain(bx, n_x, x)
    entry = cadd(inside, cmul(passing, beyond))
    for h in range(2):
        e = (entry[0][h : h + 1], entry[1][h : h + 1])
        lo, hi = slice(256 * h, 256 * h + 128), slice(256 * h + 128, 256 * h + 256)
        add = cmul(e, (qc[:, lo], qc[:, hi]))
        gc[:, lo] += add[0]
        gc[:, hi] += add[1]

    def half(k):
        return pl.ds(pl.multiple_of(k * 256, 256), 256)

    def slab(k):
        return pl.ds(pl.multiple_of(k * (BS // n_x), BS // n_x), BS // n_x)

    to_core = remote(gc.at[:, half(1 - core)], rcore, css.at[0], csr.at[0], sibling)
    to_core.start()

    for h in range(2):
        e = (entry[0][h : h + 1], entry[1][h : h + 1])
        c = cadd((cn[2 * h], cn[2 * h + 1]), cmul(e, (un[2 * h], un[2 * h + 1])))
        hi, lo = split(jnp.concatenate(c, axis=1))
        adj = dot(hi, whi[h], NT) + dot(lo, whi[h], NT) + dot(hi, wlo[h], NT)
        gi[0, :, 256 * h : 256 * h + 256] = adj.astype(BF16)

    to_core.wait_recv()
    gsum[...] = gc[:, half(core)] + rcore[...]
    to_x = []
    for d in range(1, n_x):
        k = lax.rem(x + d, n_x)
        to_x.append(remote(gsum.at[slab(k)], rx.at[x], xss.at[d], xsr.at[d], {"x": k}))
        to_x[-1].start()
    rx[x] = gsum[slab(x), :]
    for copy in to_x:
        copy.wait_recv()
    rz[z] = jnp.sum(rx[...], axis=0)
    to_z = [remote(rz.at[z], rz.at[z], zss.at[d], zsr.at[d], at_z(d)) for d in range(1, n_z)]
    for copy in to_z:
        copy.start()
    for copy in to_z:
        copy.wait_recv()
    gr[slab(x), half(core)] = jnp.sum(rz[...], axis=0)
    mine = gr.at[slab(x), half(core)]
    back_x = [remote(mine, mine, xas.at[d], xar.at[d], at_x(d)) for d in range(1, n_x)]
    for copy in back_x:
        copy.start()
    for copy in back_x:
        copy.wait_recv()
    ours = gr.at[:, half(core)]
    back_core = remote(ours, ours, cas.at[0], car.at[0], sibling)
    back_core.start()
    back_core.wait_recv()
    for h in range(2):
        hi, lo = split(gr[:, 256 * h : 256 * h + 256])
        out = dot(whi[h], hi, NT) + dot(whi[h], lo, NT) + dot(wlo[h], hi, NT)
        gt[4 * h : 4 * h + 4] = out.reshape(4, BS, BS)

    for copy in a2a + zcopies + xcopies + to_x + to_z + back_x + [to_core, back_core]:
        copy.wait_send()


def body(sizes, out_grad, prev_state, boundary, angle_code, radius_code, reflect):
    n_zh, n_core, n_x, n_zl, n_y = sizes
    n_z = n_zh * n_zl
    slab = BS // n_x
    vmem, anywhere = pl.BlockSpec(memory_space=pltpu.VMEM), pl.BlockSpec(memory_space=pl.ANY)
    plane = pltpu.VMEM((4, TOK, 128), F32)
    dma = pltpu.SemaphoreType.DMA
    return pl.pallas_call(
        functools.partial(kernel, sizes),
        out_shape=(
            jax.ShapeDtypeStruct((1, TOK, CH), BF16),
            jax.ShapeDtypeStruct((NB, BS, BS), F32),
        ),
        in_specs=[anywhere, anywhere, vmem, vmem, vmem, vmem],
        out_specs=(vmem, vmem),
        scratch_shapes=[
            pltpu.VMEM((TOK, CH), BF16),
            pltpu.VMEM((TOK, CH), BF16),
            pltpu.VMEM((2, 256, 256), BF16),
            pltpu.VMEM((2, 256, 256), BF16),
            plane, plane, plane, plane,
            pltpu.VMEM((BS, CH), F32),
            pltpu.VMEM((BS, CH), F32),
            pltpu.VMEM((BS, CH), F32),
            pltpu.VMEM((n_zl, 8, 128), F32),
            pltpu.VMEM((n_x, 8, 128), F32),
            pltpu.VMEM((BS, 256), F32),
            pltpu.VMEM((BS, 256), F32),
            pltpu.VMEM((n_x, slab, 256), F32),
            pltpu.VMEM((n_z, slab, 256), F32),
            dma((2,)),
            dma((n_y,)), dma((n_y,)),
            dma((n_zl,)), dma((n_zl,)),
            dma((n_x,)), dma((n_x,)),
            dma((1,)), dma((1,)),
            dma((n_x,)), dma((n_x,)),
            dma((n_z,)), dma((n_z,)),
            dma((n_x,)), dma((n_x,)),
            dma((1,)), dma((1,)),
        ],
        compiler_params=pltpu.CompilerParams(
            collective_id=0, has_side_effects=True, vmem_limit_bytes=32 * 2**20
        ),
    )(out_grad, prev_state, boundary, angle_code, radius_code, reflect)


def solution(mesh):
    n_dp, n_ctx, n_y = (mesh.shape[a] for a in ("dp", "ctx", "tensor"))
    n_x = min(8, n_ctx // 2)
    sizes = (n_dp // 2, 2, n_x, n_ctx // n_x, n_y)
    fine = Mesh(mesh.devices.reshape(sizes), ("zh", "core", "x", "zl", "y"))
    in_specs = (
        P(DP, (*CTX, "y"), None),
        P(DP, CTX, "y"),
        P(DP, CTX),
        P("y", None),
        P("y", None),
        P("y", None, None),
    )
    out_specs = (P(DP, CTX, "y"), P("y", None, None))
    return jax.shard_map(
        functools.partial(body, sizes), mesh=fine, in_specs=in_specs, out_specs=out_specs, check_vma=False
    )
```

time: 489 us -> 66.8 us (0.14)
  waiting for transfers between devices: 217 us -> 0 us
  matrix products: 68.7 us -> 0 us
  Pallas kernels: 0 us -> 59.8 us
  blocking collectives: 54.5 us -> 0 us
  local copies, waits for them, and re-layouts: 59 us -> 6.07 us
  other arithmetic: 36.4 us -> 0 us
  loops' own time: 23.4 us -> 0 us
  between operations: 15.2 us -> 0.65 us
  starting transfers between devices: 10.6 us -> 0 us
    psum x1 -> x0, waiting for transfers between devices: 214 us -> none  [body(): summed = lax.psum(partial_grad, DP_CTX)]
    dot_general x88 -> x0, matrix products: 68.7 us -> none  [the longest x62 39.6 us: apply_blocks(): jnp.einsum('bxy,...by->...bx', matrix, vectors, precision=lax.Precision.H...]
    pallas_call x0 -> x1, Pallas kernels: none -> 59.8 us  [body(): pl.pallas_call(functools.partial(kernel, sizes), out_shape=(jax.ShapeDtyp...]
    all_gather x3 -> x0, blocking collectives: 54.5 us -> none  [carried_in(): pieces = jax.tree.map(lambda part: lax.all_gather(part, axis), so_far)]
    dynamic_slice x48 -> x0, local copies, waits for them, and re-layouts: 32.5 us -> none  [the longest x32 18.9 us: body(): lax.scan(entry_step, zero_vector, (starts, sub_logs), reverse=True)]
    unnamed x3 -> x0, other arithmetic: 23.5 us -> none
    another operation x3 -> x0, loops' own time: 23.4 us -> none  [the longest x1 11.4 us: body(): lax.scan(entry_step, zero_vector, (starts, sub_logs), reverse=True)]
    all_to_all x1 -> x0, starting transfers between devices: 10.3 us -> none  [body(): lax.all_to_all(out_grad, 'tensor', split_axis=2, concat_axis=1, tiled=True)]
  transfers between devices with their start and end apart: 3 -> 0, of which waited for: 2 -> 0; matrix products, arithmetic and copies ran while one was open for 19% -> 0% of each run, Pallas kernels for 0% -> 0%
where the time goes in v1:
time: 66.8 us; the launch traced here: 66.5 us
  Pallas kernels  59.8 us (90%)
  local copies, waits for them, and re-layouts  6.07 us (9%)
    pallas_call x1, Pallas kernels, body(): pl.pallas_call(functools.partial(kernel, sizes), out_shape=(jax.ShapeDtyp...  59.8 us
    unnamed x14, local copies, waits for them, and re-layouts  6.07 us

profile of v1, /device:TPU:1, one launch (start us, length us, event | category | flops | bytes accessed | tf_op | source)
XLA Modules:
  0.0 66.5 jit_solution(16171278689548137933)
XLA Ops:
  0.6 0.0 copy-start
  0.6 0.9 %copy-done = bf16[1,32,4096]{2,1,0:T(8,128)(2,1)S(1)} copy-done((bf16[1,32,4096]{2,1,0:T(8,128)(2,1)S(1)}, bf16[1,32,4096]{2,1,0:T(8,128)(2,1)}, u32[]{:S(2)}) %copy-start) | copy-done | bytes 262168
  1.6 0.0 copy-start.1
  1.6 0.9 %copy-done.1 = bf16[1,256,512]{2,1,0:T(8,128)(2,1)S(1)} copy-done((bf16[1,256,512]{2,1,0:T(8,128)(2,1)S(1)}, bf16[1,256,512]{2,1,0:T(8,128)(2,1)}, u32[]{:S(2)}) %copy-start.1) | copy-done | bytes 262168
  2.5 0.0 copy-start.2
  2.5 0.7 %copy-done.2 = f32[8,4,64]{2,1,0:T(4,128)S(1)} copy-done((f32[8,4,64]{2,1,0:T(4,128)S(1)}, f32[8,4,64]{2,1,0:T(4,128)}, u32[]{:S(2)}) %copy-start.2) | copy-done | bytes 8216
  3.3 0.0 copy-start.3
  3.3 0.7 %copy-done.3 = s32[8,32]{1,0:T(8,128)S(1)} copy-done((s32[8,32]{1,0:T(8,128)S(1)}, s32[8,32]{1,0:T(8,128)}, u32[]{:S(2)}) %copy-start.3) | copy-done | bytes 1048
  3.9 0.0 copy-start.4
  3.9 0.7 %copy-done.4 = s32[8,32]{1,0:T(8,128)S(1)} copy-done((s32[8,32]{1,0:T(8,128)S(1)}, s32[8,32]{1,0:T(8,128)}, u32[]{:S(2)}) %copy-start.4) | copy-done | bytes 1048
  4.6 0.0 copy-start.5
  4.6 0.7 %copy-done.5 = s32[1,256]{1,0:T(1,128)S(1)} copy-done((s32[1,256]{1,0:T(1,128)S(1)}, s32[1,256]{1,0:T(1,128)}, u32[]{:S(2)}) %copy-start.5) | copy-done | bytes 1048
  5.3 59.8 %shard_map.77 = (bf16[1,256,512]{2,1,0:T(8,128)(2,1)S(1)}, f32[8,64,64]{2,1,0:T(8,128)S(1)}) custom-call(bf16[1,32,4096]{2,1,0:T(8,128)(2,1)S(1)} %copy-done, bf16[1,256,512]{2,1,0:T(8,128)(2,1)S(1)} %copy-done.1, s32[1,256]{1,0:T(1,128)S(1)} %copy-done.5, s32[8,32]{1,0:T(8,128)S(1)} %copy-done.3, s32[8,32]{1,0:T(8,128)S(1)} %copy-done.4, ...), custom_call_target="tpu_custom_call" | custom-call | tf_op jit(solution)/shard_map/pallas_call | solution.py:356
  65.1 0.7 %copy.10 = bf16[1,256,512]{2,1,0:T(8,128)(2,1)} copy(bf16[1,256,512]{2,1,0:T(8,128)(2,1)S(1)} %get-tuple-element.4) | data formatting | bytes 524288
  65.8 0.7 %copy.11 = f32[8,64,64]{2,1,0:T(8,128)} copy(f32[8,64,64]{2,1,0:T(8,128)S(1)} %get-tuple-element.5) | data formatting | bytes 262144
Async XLA Ops:
  0.6 1.0 %copy-start = (bf16[1,32,4096]{2,1,0:T(8,128)(2,1)S(1)}, bf16[1,32,4096]{2,1,0:T(8,128)(2,1)}, u32[]{:S(2)}) copy-start(bf16[1,32,4096]{2,1,0:T(8,128)(2,1)} %og.1) | copy-start | bytes 786436
  1.6 0.9 %copy-start.1 = (bf16[1,256,512]{2,1,0:T(8,128)(2,1)S(1)}, bf16[1,256,512]{2,1,0:T(8,128)(2,1)}, u32[]{:S(2)}) copy-start(bf16[1,256,512]{2,1,0:T(8,128)(2,1)} %ps.1) | copy-start | bytes 786436
  2.5 0.7 %copy-start.2 = (f32[8,4,64]{2,1,0:T(4,128)S(1)}, f32[8,4,64]{2,1,0:T(4,128)}, u32[]{:S(2)}) copy-start(f32[8,4,64]{2,1,0:T(4,128)} %rf.1) | copy-start | bytes 24580
  3.3 0.7 %copy-start.3 = (s32[8,32]{1,0:T(8,128)S(1)}, s32[8,32]{1,0:T(8,128)}, u32[]{:S(2)}) copy-start(s32[8,32]{1,0:T(8,128)} %ac.1) | copy-start | bytes 3076
  3.9 0.7 %copy-start.4 = (s32[8,32]{1,0:T(8,128)S(1)}, s32[8,32]{1,0:T(8,128)}, u32[]{:S(2)}) copy-start(s32[8,32]{1,0:T(8,128)} %rc.1) | copy-start | bytes 3076
  4.6 0.7 %copy-start.5 = (s32[1,256]{1,0:T(1,128)S(1)}, s32[1,256]{1,0:T(1,128)}, u32[]{:S(2)}) copy-start(s32[1,256]{1,0:T(1,128)} %bd.1) | copy-start | bytes 3076

commit v2 on v1

--- a/solution.py
+++ b/solution.py
@@ -59,9 +59,9 @@
 
 
 def kernel(
-    sizes, og, ps, bd, ac, rc, rf, gi, gt,
-    g, pv, whi, wlo, kl, wq, un, cn, qc, gc, gr, bz, bx, gsum, rcore, rx, rz,
-    lsem, ysend, yrecv, bzs, bzr, bxs, bxr, css, csr, xss, xsr, zss, zsr, xas, xar, cas, car,
+    sizes, og, ps, bd_in, ac_in, rc_in, rf_in, gi, gt,
+    bd, ac, rc, rf, g, pv, whi, wlo, kl, wq, un, cn, qc, rq, gc, gr, bz, bx, gsum, rcore, rx, eq, req, rz,
+    lsem, ysend, yrecv, qss, qsr, bzs, bzr, bxs, bxr, css, csr, xss, xsr, zss, zsr, xas, xar,
 ):
     n_zh, n_core, n_x, n_zl, n_y = sizes
     n_z = n_zh * n_zl
@@ -98,6 +98,12 @@
             src_ref=src, dst_ref=dst, send_sem=send, recv_sem=recv, device_id=where, device_id_type=MESH
         )
 
+    small = [
+        pltpu.make_async_copy(src, dst, lsem.at[2 + i])
+        for i, (src, dst) in enumerate(((ac_in, ac), (rc_in, rc), (bd_in, bd), (rf_in, rf)))
+    ]
+    for copy in small:
+        copy.start()
     load_prev = pltpu.make_async_copy(ps.at[0], pv, lsem.at[0])
     load_prev.start()
     own_rows = pl.ds(pl.multiple_of(y * rows, rows), rows)
@@ -118,6 +124,8 @@
         )
         a2a[-1].start()
 
+    for copy in small:
+        copy.wait()
     pick = (iota((32, 128), 1) % 32 == iota((32, 128), 0)).astype(F32)
     acode = fdot(ac[...].astype(F32), pick, NN)
     rcode = fdot(rc[...].astype(F32), pick, NN)
@@ -213,9 +221,25 @@
         hi, lo = split(jnp.concatenate([ref[2 * h], ref[2 * h + 1]], axis=1))
         return compact(dot(prev, hi, TN) + dot(prev, lo, TN))
 
+    def half(k):
+        return pl.ds(pl.multiple_of(k * 256, 256), 256)
+
+    def slab(k):
+        return pl.ds(pl.multiple_of(k * (BS // n_x), BS // n_x), BS // n_x)
+
+    def scatter_x(src, dst, send, recv):
+        copies = []
+        for d in range(1, n_x):
+            k = lax.rem(x + d, n_x)
+            copies.append(remote(src.at[slab(k)], dst.at[x], send.at[d], recv.at[d], {"x": k}))
+            copies[-1].start()
+        dst[x] = src[slab(x), :]
+        return copies
+
     load_prev.wait()
     for h in range(2):
         qc[:, 256 * h : 256 * h + 256] = with_prev(un, h)
+    to_q = scatter_x(qc, rq, qss, qsr)
 
     load_own.wait()
     for copy in a2a:
@@ -255,75 +279,68 @@
         return 0
 
     lax.fori_loop(0, STEP // 4, fix, 0)
+    for h in range(2):
+        gc[:, 256 * h : 256 * h + 256] = with_prev(cn, h)
+    to_core = remote(gc.at[:, half(1 - core)], rcore, css.at[0], csr.at[0], sibling)
+    to_core.start()
     for copy in zcopies:
         copy.wait_recv()
 
-    def firsts(ref, j):
-        return ((ref[j, 0:2, :], ref[j, 2:4, :]), (ref[j, 4:6, :], ref[j, 6:8, :]))
+    def pair(ref, j, at):
+        return ref[j, at : at + 2, :], ref[j, at + 2 : at + 4, :]
 
     zero2 = (jnp.zeros((2, 128), F32), jnp.zeros((2, 128), F32))
     one2 = (jnp.ones((2, 128), F32), jnp.zeros((2, 128), F32))
-
-    def chain(ref, count, me):
-        inside, passing = zero2, one2
-        total, span = zero2, one2
-        for j in reversed(range(count)):
-            f, m = firsts(ref, j)
-            total, span = cadd(f, cmul(m, total)), cmul(m, span)
-            inside = cwhere(j > me, total, inside)
-            passing = cwhere(j > me, span, passing)
-        return inside, passing, total, span
-
-    inside, passing, total, span = chain(bz, n_zl, zl)
-    for part in range(2):
-        bx[x, 2 * part : 2 * part + 2, :] = total[part]
-        bx[x, 4 + 2 * part : 6 + 2 * part, :] = span[part]
+    inside, passing, total, span = zero2, one2, zero2, one2
+    for j in reversed(range(n_zl)):
+        inside, passing = cwhere(j == zl, total, inside), cwhere(j == zl, span, passing)
+        f, m = pair(bz, j, 0), pair(bz, j, 4)
+        total, span = cadd(f, cmul(m, total)), cmul(m, span)
+    for i, value in enumerate((total, span, inside, passing)):
+        for part in range(2):
+            bx[x, 4 * i + 2 * part : 4 * i + 2 * part + 2, :] = value[part]
     xcopies = [remote(bx.at[x], bx.at[x], bxs.at[d], bxr.at[d], at_x(d)) for d in range(1, n_x)]
     for copy in xcopies:
         copy.start()
-    for h in range(2):
-        gc[:, 256 * h : 256 * h + 256] = with_prev(cn, h)
+    to_core.wait_recv()
+    gsum[...] = gc[:, half(core)] + rcore[...]
+    to_x = scatter_x(gsum, rx, xss, xsr)
+    for copy in to_q:
+        copy.wait_recv()
     for copy in xcopies:
         copy.wait_recv()
-    beyond, _, _, _ = chain(bx, n_x, x)
-    entry = cadd(inside, cmul(passing, beyond))
-    for h in range(2):
-        e = (entry[0][h : h + 1], entry[1][h : h + 1])
-        lo, hi = slice(256 * h, 256 * h + 128), slice(256 * h + 128, 256 * h + 256)
-        add = cmul(e, (qc[:, lo], qc[:, hi]))
-        gc[:, lo] += add[0]
-        gc[:, hi] += add[1]
-
-    def half(k):
-        return pl.ds(pl.multiple_of(k * 256, 256), 256)
-
-    def slab(k):
-        return pl.ds(pl.multiple_of(k * (BS // n_x), BS // n_x), BS // n_x)
-
-    to_core = remote(gc.at[:, half(1 - core)], rcore, css.at[0], csr.at[0], sibling)
-    to_core.start()
-
+
+    beyond, entry = zero2, zero2
+    sums = [zero, zero]
+    for j in reversed(range(n_x)):
+        here = cadd(pair(bx, j, 8), cmul(pair(bx, j, 12), beyond))
+        entry = cwhere(j == x, here, entry)
+        beyond = cadd(pair(bx, j, 0), cmul(pair(bx, j, 4), beyond))
+        for h in range(2):
+            e = (here[0][h : h + 1], here[1][h : h + 1])
+            weight = (rq[j, :, 256 * h : 256 * h + 128], rq[j, :, 256 * h + 128 : 256 * h + 256])
+            term = cmul(e, weight)
+            sums[h] = term if j == n_x - 1 else cadd(sums[h], term)
+    for h in range(2):
+        for part in range(2):
+            at = 256 * h + 128 * part
+            eq[:, at : at + 128] = sums[h][part]
+    to_core_2 = remote(eq.at[:, half(1 - core)], req, css.at[1], csr.at[1], sibling)
+    to_core_2.start()
+    for copy in to_x:
+        copy.wait_recv()
+    owned = jnp.sum(rx[...], axis=0) + eq[:, half(core)]
+    to_core_2.wait_recv()
+    rz[z] = owned + req[...]
+    to_z = [remote(rz.at[z], rz.at[z], zss.at[d], zsr.at[d], at_z(d)) for d in range(1, n_z)]
+    for copy in to_z:
+        copy.start()
     for h in range(2):
         e = (entry[0][h : h + 1], entry[1][h : h + 1])
         c = cadd((cn[2 * h], cn[2 * h + 1]), cmul(e, (un[2 * h], un[2 * h + 1])))
         hi, lo = split(jnp.concatenate(c, axis=1))
         adj = dot(hi, whi[h], NT) + dot(lo, whi[h], NT) + dot(hi, wlo[h], NT)
         gi[0, :, 256 * h : 256 * h + 256] = adj.astype(BF16)
-
-    to_core.wait_recv()
-    gsum[...] = gc[:, half(core)] + rcore[...]
-    to_x = []
-    for d in range(1, n_x):
-        k = lax.rem(x + d, n_x)
-        to_x.append(remote(gsum.at[slab(k)], rx.at[x], xss.at[d], xsr.at[d], {"x": k}))
-        to_x[-1].start()
-    rx[x] = gsum[slab(x), :]
-    for copy in to_x:
-        copy.wait_recv()
-    rz[z] = jnp.sum(rx[...], axis=0)
-    to_z = [remote(rz.at[z], rz.at[z], zss.at[d], zsr.at[d], at_z(d)) for d in range(1, n_z)]
-    for copy in to_z:
-        copy.start()
     for copy in to_z:
         copy.wait_recv()
     gr[slab(x), half(core)] = jnp.sum(rz[...], axis=0)
@@ -334,23 +351,27 @@
     for copy in back_x:
         copy.wait_recv()
     ours = gr.at[:, half(core)]
-    back_core = remote(ours, ours, cas.at[0], car.at[0], sibling)
+    back_core = remote(ours, ours, css.at[2], csr.at[2], sibling)
     back_core.start()
+
+    def finish(h):
+        hi, lo = split(gr[:, half(h)])
+        out = dot(whi[h], hi, NT) + dot(whi[h], lo, NT) + dot(wlo[h], hi, NT)
+        gt[pl.ds(4 * h, 4)] = out.reshape(4, BS, BS)
+
+    finish(core)
     back_core.wait_recv()
-    for h in range(2):
-        hi, lo = split(gr[:, 256 * h : 256 * h + 256])
-        out = dot(whi[h], hi, NT) + dot(whi[h], lo, NT) + dot(wlo[h], hi, NT)
-        gt[4 * h : 4 * h + 4] = out.reshape(4, BS, BS)
-
-    for copy in a2a + zcopies + xcopies + to_x + to_z + back_x + [to_core, back_core]:
+    finish(1 - core)
+
+    for copy in a2a + to_q + zcopies + [to_core] + xcopies + to_x + [to_core_2] + to_z + back_x + [back_core]:
         copy.wait_send()
 
 
-def body(sizes, out_grad, prev_state, boundary, angle_code, radius_code, reflect):
+def body(sizes, *operands):
     n_zh, n_core, n_x, n_zl, n_y = sizes
     n_z = n_zh * n_zl
     slab = BS // n_x
-    vmem, anywhere = pl.BlockSpec(memory_space=pltpu.VMEM), pl.BlockSpec(memory_space=pl.ANY)
+    vmem, anywhere = pl.BlockSpec(memory_space=pltpu.VMEM), pl.BlockSpec(memory_space=pltpu.HBM)
     plane = pltpu.VMEM((4, TOK, 128), F32)
     dma = pltpu.SemaphoreType.DMA
     return pl.pallas_call(
@@ -359,37 +380,44 @@
             jax.ShapeDtypeStruct((1, TOK, CH), BF16),
             jax.ShapeDtypeStruct((NB, BS, BS), F32),
         ),
-        in_specs=[anywhere, anywhere, vmem, vmem, vmem, vmem],
+        in_specs=[anywhere] * 6,
         out_specs=(vmem, vmem),
         scratch_shapes=[
+            pltpu.VMEM((1, TOK), I32),
+            pltpu.VMEM((NB, 32), I32),
+            pltpu.VMEM((NB, 32), I32),
+            pltpu.VMEM((NB, 4, BS), F32),
             pltpu.VMEM((TOK, CH), BF16),
             pltpu.VMEM((TOK, CH), BF16),
             pltpu.VMEM((2, 256, 256), BF16),
             pltpu.VMEM((2, 256, 256), BF16),
             plane, plane, plane, plane,
             pltpu.VMEM((BS, CH), F32),
+            pltpu.VMEM((n_x, slab, CH), F32),
             pltpu.VMEM((BS, CH), F32),
             pltpu.VMEM((BS, CH), F32),
             pltpu.VMEM((n_zl, 8, 128), F32),
-            pltpu.VMEM((n_x, 8, 128), F32),
+            pltpu.VMEM((n_x, 16, 128), F32),
             pltpu.VMEM((BS, 256), F32),
             pltpu.VMEM((BS, 256), F32),
             pltpu.VMEM((n_x, slab, 256), F32),
+            pltpu.VMEM((slab, CH), F32),
+            pltpu.VMEM((slab, 256), F32),
             pltpu.VMEM((n_z, slab, 256), F32),
-            dma((2,)),
+            dma((6,)),
             dma((n_y,)), dma((n_y,)),
+            dma((n_x,)), dma((n_x,)),
             dma((n_zl,)), dma((n_zl,)),
             dma((n_x,)), dma((n_x,)),
-            dma((1,)), dma((1,)),
+            dma((3,)), dma((3,)),
             dma((n_x,)), dma((n_x,)),
             dma((n_z,)), dma((n_z,)),
             dma((n_x,)), dma((n_x,)),
-            dma((1,)), dma((1,)),
         ],
         compiler_params=pltpu.CompilerParams(
             collective_id=0, has_side_effects=True, vmem_limit_bytes=32 * 2**20
         ),
-    )(out_grad, prev_state, boundary, angle_code, radius_code, reflect)
+    )(*(pltpu.with_memory_space_constraint(a, pltpu.HBM) for a in operands))
 
 
 def solution(mesh):

time: 66.8 us -> 59.2 us (0.89)
  local copies, waits for them, and re-layouts: 6.07 us -> 1.41 us
  Pallas kernels: 59.8 us -> 57 us
    unnamed x14 -> x2, local copies, waits for them, and re-layouts: 6.07 us -> 1.41 us
    pallas_call x1, Pallas kernels: 59.8 us -> 57 us  [body(): pl.pallas_call(functools.partial(kernel, sizes), out_shape=(jax.ShapeDtyp...]
where the time goes in v2:
time: 59.2 us; the launch traced here: 59.1 us
  Pallas kernels  57 us (96%)
  local copies, waits for them, and re-layouts  1.41 us (2%)
  between operations  0.64 us (1%)
    pallas_call x1, Pallas kernels, body(): pl.pallas_call(functools.partial(kernel, sizes), out_shape=(jax.ShapeDtyp...  57 us
    unnamed x2, local copies, waits for them, and re-layouts  1.41 us

profile of v2, /device:TPU:1, one launch (start us, length us, event | category | flops | bytes accessed | tf_op | source)
XLA Modules:
  0.0 59.1 jit_solution(10184517437687172605)
XLA Ops:
  0.6 57.0 %shard_map.77 = (bf16[1,256,512]{2,1,0:T(8,128)(2,1)S(1)}, f32[8,64,64]{2,1,0:T(8,128)S(1)}) custom-call(bf16[1,32,4096]{2,1,0:T(8,128)(2,1)} %og.1, bf16[1,256,512]{2,1,0:T(8,128)(2,1)} %ps.1, s32[1,256]{1,0:T(1,128)} %bd_in.1, s32[8,32]{1,0:T(8,128)} %ac_in.1, s32[8,32]{1,0:T(8,128)} %rc_in.1, f32[8,4,64]{2,1,0:T(4,128)} %rf_in.1), custom_call_target="tpu_custom_call" | custom-call | tf_op jit(solution)/shard_map/pallas_call | solution.py:377
  57.7 0.7 %copy.10 = bf16[1,256,512]{2,1,0:T(8,128)(2,1)} copy(bf16[1,256,512]{2,1,0:T(8,128)(2,1)S(1)} %get-tuple-element.4) | data formatting | bytes 524288
  58.4 0.7 %copy.11 = f32[8,64,64]{2,1,0:T(8,128)} copy(f32[8,64,64]{2,1,0:T(8,128)S(1)} %get-tuple-element.5) | data formatting | bytes 262144

commit v3 on v2

--- a/solution.py
+++ b/solution.py
@@ -50,6 +50,10 @@
     return jnp.where(m, a[0], b[0]), jnp.where(m, a[1], b[1])
 
 
+def far_first(count):
+    return sorted(range(1, count), key=lambda d: -min(d, count - d))
+
+
 def compact(full):
     lane_block = (iota((BS, 256), 1) % 128) // 32
     out = jnp.zeros((BS, 256), F32)
@@ -60,8 +64,8 @@
 
 def kernel(
     sizes, og, ps, bd_in, ac_in, rc_in, rf_in, gi, gt,
-    bd, ac, rc, rf, g, pv, whi, wlo, kl, wq, un, cn, qc, rq, gc, gr, bz, bx, gsum, rcore, rx, eq, req, rz,
-    lsem, ysend, yrecv, qss, qsr, bzs, bzr, bxs, bxr, css, csr, xss, xsr, zss, zsr, xas, xar,
+    bd, ac, rc, rf, g, pv, whi, wlo, kl, wq, un, cn, qc, rq, gc, gr, bc, gsum, rcore, rx, eq, req, rz,
+    lsem, ysend, yrecv, qss, qsr, bcs, bcr, css, csr, xss, xsr, zss, zsr, xas, xar, ready,
 ):
     n_zh, n_core, n_x, n_zl, n_y = sizes
     n_z = n_zh * n_zl
@@ -79,8 +83,8 @@
         k = lax.rem(z + d, n_z)
         return {"zh": k // n_zl, "zl": lax.rem(k, n_zl)}
 
-    def at_zl(d):
-        return {"zl": lax.rem(zl + d, n_zl)}
+    def at_ctx(d, e):
+        return {"x": lax.rem(x + d, n_x), "zl": lax.rem(zl + e, n_zl)}
 
     sibling = {"core": 1 - core}
     partners = (
@@ -112,6 +116,8 @@
     )
     load_own.start()
     pl.semaphore_wait(barrier, len(partners))
+    for d in range(1, n_x):
+        pl.semaphore_signal(ready, inc=1, device_id=at_x(d), device_id_type=MESH)
 
     a2a = []
     for d in range(1, n_y):
@@ -224,12 +230,15 @@
     def half(k):
         return pl.ds(pl.multiple_of(k * 256, 256), 256)
 
+    n_own = n_x // 2
+    deep = BS // n_own
+
     def slab(k):
-        return pl.ds(pl.multiple_of(k * (BS // n_x), BS // n_x), BS // n_x)
+        return pl.ds(pl.multiple_of(lax.rem(k, n_own) * deep, deep), deep)
 
     def scatter_x(src, dst, send, recv):
         copies = []
-        for d in range(1, n_x):
+        for d in far_first(n_x):
             k = lax.rem(x + d, n_x)
             copies.append(remote(src.at[slab(k)], dst.at[x], send.at[d], recv.at[d], {"x": k}))
             copies[-1].start()
@@ -258,18 +267,23 @@
         return c
 
     first = lax.fori_loop(0, STEP // 4, back, [zero, zero])
-    entering = []
+    entering, me = [], x * n_zl + zl
     for h in range(2):
         v = first[h]
         for m, step in zip((1, 2, 4), hops[h]):
             v = cadd(v, cmul(step, later(v, m)))
         entering.append(cwhere(sub < SUB - 1, later(v, 1), zero))
         for part in range(2):
-            bz[zl, 2 * part + h : 2 * part + h + 1, :] = v[part][0:1]
-            bz[zl, 4 + 2 * part + h : 5 + 2 * part + h, :] = mu[h][part]
-
-    zcopies = [remote(bz.at[zl], bz.at[zl], bzs.at[d], bzr.at[d], at_zl(d)) for d in range(1, n_zl)]
-    for copy in zcopies:
+            bc[me, 2 * part + h : 2 * part + h + 1, :] = v[part][0:1]
+            bc[me, 4 + 2 * part + h : 5 + 2 * part + h, :] = mu[h][part]
+
+    pl.semaphore_wait(ready, n_x - 1)
+    offsets = [(d, e) for d in range(n_x) for e in range(n_zl) if d or e]
+    offsets.sort(key=lambda o: -min(o[0], n_x - o[0]) - min(o[1], n_zl - o[1]))
+    carries = [
+        remote(bc.at[me], bc.at[me], bcs.at[i], bcr.at[i], at_ctx(*o)) for i, o in enumerate(offsets)
+    ]
+    for copy in carries:
         copy.start()
 
     def fix(i, _):
@@ -283,39 +297,34 @@
         gc[:, 256 * h : 256 * h + 256] = with_prev(cn, h)
     to_core = remote(gc.at[:, half(1 - core)], rcore, css.at[0], csr.at[0], sibling)
     to_core.start()
-    for copy in zcopies:
-        copy.wait_recv()
-
-    def pair(ref, j, at):
-        return ref[j, at : at + 2, :], ref[j, at + 2 : at + 4, :]
-
-    zero2 = (jnp.zeros((2, 128), F32), jnp.zeros((2, 128), F32))
-    one2 = (jnp.ones((2, 128), F32), jnp.zeros((2, 128), F32))
-    inside, passing, total, span = zero2, one2, zero2, one2
-    for j in reversed(range(n_zl)):
-        inside, passing = cwhere(j == zl, total, inside), cwhere(j == zl, span, passing)
-        f, m = pair(bz, j, 0), pair(bz, j, 4)
-        total, span = cadd(f, cmul(m, total)), cmul(m, span)
-    for i, value in enumerate((total, span, inside, passing)):
-        for part in range(2):
-            bx[x, 4 * i + 2 * part : 4 * i + 2 * part + 2, :] = value[part]
-    xcopies = [remote(bx.at[x], bx.at[x], bxs.at[d], bxr.at[d], at_x(d)) for d in range(1, n_x)]
-    for copy in xcopies:
-        copy.start()
     to_core.wait_recv()
     gsum[...] = gc[:, half(core)] + rcore[...]
     to_x = scatter_x(gsum, rx, xss, xsr)
     for copy in to_q:
         copy.wait_recv()
-    for copy in xcopies:
-        copy.wait_recv()
-
+    for copy in carries:
+        copy.wait_recv()
+
+    def pair(j, at):
+        return bc[j, at : at + 2, :], bc[j, at + 2 : at + 4, :]
+
+    zero2 = (jnp.zeros((2, 128), F32), jnp.zeros((2, 128), F32))
+    one2 = (jnp.ones((2, 128), F32), jnp.zeros((2, 128), F32))
+    chains = []
+    for k in range(n_x):
+        inside, passing, total, span = zero2, one2, zero2, one2
+        for j in reversed(range(n_zl)):
+            inside, passing = cwhere(j == zl, total, inside), cwhere(j == zl, span, passing)
+            f, m = pair(k * n_zl + j, 0), pair(k * n_zl + j, 4)
+            total, span = cadd(f, cmul(m, total)), cmul(m, span)
+        chains.append((inside, passing, total, span))
     beyond, entry = zero2, zero2
     sums = [zero, zero]
     for j in reversed(range(n_x)):
-        here = cadd(pair(bx, j, 8), cmul(pair(bx, j, 12), beyond))
+        inside, passing, total, span = chains[j]
+        here = cadd(inside, cmul(passing, beyond))
         entry = cwhere(j == x, here, entry)
-        beyond = cadd(pair(bx, j, 0), cmul(pair(bx, j, 4), beyond))
+        beyond = cadd(total, cmul(span, beyond))
         for h in range(2):
             e = (here[0][h : h + 1], here[1][h : h + 1])
             weight = (rq[j, :, 256 * h : 256 * h + 128], rq[j, :, 256 * h + 128 : 256 * h + 256])
@@ -332,7 +341,7 @@
     owned = jnp.sum(rx[...], axis=0) + eq[:, half(core)]
     to_core_2.wait_recv()
     rz[z] = owned + req[...]
-    to_z = [remote(rz.at[z], rz.at[z], zss.at[d], zsr.at[d], at_z(d)) for d in range(1, n_z)]
+    to_z = [remote(rz.at[z], rz.at[z], zss.at[d], zsr.at[d], at_z(d)) for d in far_first(n_z)]
     for copy in to_z:
         copy.start()
     for h in range(2):
@@ -343,11 +352,14 @@
         gi[0, :, 256 * h : 256 * h + 256] = adj.astype(BF16)
     for copy in to_z:
         copy.wait_recv()
-    gr[slab(x), half(core)] = jnp.sum(rz[...], axis=0)
+    hi, lo = split(jnp.sum(rz[...], axis=0))
+    gr[slab(x), half(core)] = dot(hi, whi[core], NT) + dot(lo, whi[core], NT) + dot(hi, wlo[core], NT)
     mine = gr.at[slab(x), half(core)]
-    back_x = [remote(mine, mine, xas.at[d], xar.at[d], at_x(d)) for d in range(1, n_x)]
-    for copy in back_x:
-        copy.start()
+    back_x = []
+    for i, d in enumerate(far_first(n_own)):
+        where = at_x(d if d <= n_own // 2 else n_x - n_own + d)
+        back_x.append(remote(mine, mine, xas.at[i], xar.at[i], where))
+        back_x[-1].start()
     for copy in back_x:
         copy.wait_recv()
     ours = gr.at[:, half(core)]
@@ -355,22 +367,20 @@
     back_core.start()
 
     def finish(h):
-        hi, lo = split(gr[:, half(h)])
-        out = dot(whi[h], hi, NT) + dot(whi[h], lo, NT) + dot(wlo[h], hi, NT)
-        gt[pl.ds(4 * h, 4)] = out.reshape(4, BS, BS)
+        gt[pl.ds(4 * h, 4)] = gr[:, half(h)].T.reshape(4, BS, BS)
 
     finish(core)
     back_core.wait_recv()
     finish(1 - core)
 
-    for copy in a2a + to_q + zcopies + [to_core] + xcopies + to_x + [to_core_2] + to_z + back_x + [back_core]:
+    for copy in a2a + to_q + carries + [to_core] + to_x + [to_core_2] + to_z + back_x + [back_core]:
         copy.wait_send()
 
 
 def body(sizes, *operands):
     n_zh, n_core, n_x, n_zl, n_y = sizes
     n_z = n_zh * n_zl
-    slab = BS // n_x
+    slab = BS // (n_x // 2)
     vmem, anywhere = pl.BlockSpec(memory_space=pltpu.VMEM), pl.BlockSpec(memory_space=pltpu.HBM)
     plane = pltpu.VMEM((4, TOK, 128), F32)
     dma = pltpu.SemaphoreType.DMA
@@ -396,8 +406,7 @@
             pltpu.VMEM((n_x, slab, CH), F32),
             pltpu.VMEM((BS, CH), F32),
             pltpu.VMEM((BS, CH), F32),
-            pltpu.VMEM((n_zl, 8, 128), F32),
-            pltpu.VMEM((n_x, 16, 128), F32),
+            pltpu.VMEM((n_x * n_zl, 8, 128), F32),
             pltpu.VMEM((BS, 256), F32),
             pltpu.VMEM((BS, 256), F32),
             pltpu.VMEM((n_x, slab, 256), F32),
@@ -407,12 +416,12 @@
             dma((6,)),
             dma((n_y,)), dma((n_y,)),
             dma((n_x,)), dma((n_x,)),
-            dma((n_zl,)), dma((n_zl,)),
-            dma((n_x,)), dma((n_x,)),
+            dma((n_x * n_zl,)), dma((n_x * n_zl,)),
             dma((3,)), dma((3,)),
             dma((n_x,)), dma((n_x,)),
             dma((n_z,)), dma((n_z,)),
             dma((n_x,)), dma((n_x,)),
+            pltpu.SemaphoreType.REGULAR,
         ],
         compiler_params=pltpu.CompilerParams(
             collective_id=0, has_side_effects=True, vmem_limit_bytes=32 * 2**20

time: 59.2 us -> 56 us (0.946)
  Pallas kernels: 57 us -> 53.8 us
    pallas_call x1, Pallas kernels: 57 us -> 53.8 us  [body(): pl.pallas_call(functools.partial(kernel, sizes), out_shape=(jax.ShapeDtyp...]
where the time goes in v3:
time: 56 us; the launch traced here: 55.8 us
  Pallas kernels  53.8 us (96%)
  local copies, waits for them, and re-layouts  1.41 us (3%)
  between operations  0.64 us (1%)
    pallas_call x1, Pallas kernels, body(): pl.pallas_call(functools.partial(kernel, sizes), out_shape=(jax.ShapeDtyp...  53.8 us
    unnamed x2, local copies, waits for them, and re-layouts  1.41 us

profile of v3, /device:TPU:1, one launch (start us, length us, event | category | flops | bytes accessed | tf_op | source)
XLA Modules:
  0.0 55.8 jit_solution(13753118214556624706)
XLA Ops:
  0.6 53.8 %shard_map.77 = (bf16[1,256,512]{2,1,0:T(8,128)(2,1)S(1)}, f32[8,64,64]{2,1,0:T(8,128)S(1)}) custom-call(bf16[1,32,4096]{2,1,0:T(8,128)(2,1)} %og.1, bf16[1,256,512]{2,1,0:T(8,128)(2,1)} %ps.1, s32[1,256]{1,0:T(1,128)} %bd_in.1, s32[8,32]{1,0:T(8,128)} %ac_in.1, s32[8,32]{1,0:T(8,128)} %rc_in.1, f32[8,4,64]{2,1,0:T(4,128)} %rf_in.1), custom_call_target="tpu_custom_call" | custom-call | tf_op jit(solution)/shard_map/pallas_call | solution.py:387
  54.4 0.7 %copy.10 = bf16[1,256,512]{2,1,0:T(8,128)(2,1)} copy(bf16[1,256,512]{2,1,0:T(8,128)(2,1)S(1)} %get-tuple-element.4) | data formatting | bytes 524288
  55.1 0.7 %copy.11 = f32[8,64,64]{2,1,0:T(8,128)} copy(f32[8,64,64]{2,1,0:T(8,128)S(1)} %get-tuple-element.5) | data formatting | bytes 262144

commit v4 on v3

--- a/solution.py
+++ b/solution.py
@@ -64,7 +64,7 @@
 
 def kernel(
     sizes, og, ps, bd_in, ac_in, rc_in, rf_in, gi, gt,
-    bd, ac, rc, rf, g, pv, whi, wlo, kl, wq, un, cn, qc, rq, gc, gr, bc, gsum, rcore, rx, eq, req, rz,
+    bd, ac, rc, rf, g, pv, whi, wlo, kl, wq, fw, un, cn, qc, rq, gc, gr, bc, gsum, rcore, rx, eq, req, rz,
     lsem, ysend, yrecv, qss, qsr, bcs, bcr, css, csr, xss, xsr, zss, zsr, xas, xar, ready,
 ):
     n_zh, n_core, n_x, n_zl, n_y = sizes
@@ -88,9 +88,9 @@
 
     sibling = {"core": 1 - core}
     partners = (
-        [at_y(d) for d in range(1, n_y)]
-        + [at_x(d) for d in range(1, n_x)]
-        + [at_z(d) for d in range(1, n_z)]
+        [at_y(d) for d in far_first(n_y)]
+        + [at_x(d) for d in far_first(n_x)]
+        + [at_z(d) for d in far_first(n_z)]
         + [sibling]
     )
     barrier = pltpu.get_barrier_semaphore()
@@ -115,6 +115,32 @@
         og.at[0, :, pl.ds(pl.multiple_of(y * CH, CH), CH)], g.at[own_rows], lsem.at[1]
     )
     load_own.start()
+    for copy in small:
+        copy.wait()
+    pick = (iota((32, 128), 1) % 32 == iota((32, 128), 0)).astype(F32)
+    acode = fdot(ac[...].astype(F32), pick, NN)
+    rcode = fdot(rc[...].astype(F32), pick, NN)
+    radius = 1.0 - jnp.exp2(-(4.0 + rcode * (10.0 / 1024.0)))
+    angle = acode * (math.pi / 4096.0)
+    lam_r, lam_i = radius * jnp.cos(angle), -radius * jnp.sin(angle)
+    lam = []
+    for h in range(2):
+        mine = iota((NB, 128), 0) == 4 * h + iota((NB, 128), 1) // 32
+        lam.append(
+            tuple(
+                jnp.broadcast_to(jnp.sum(jnp.where(mine, v, 0.0), axis=0, keepdims=True), (SUB, 128))
+                for v in (lam_r, lam_i)
+            )
+        )
+
+    r_id, t_id = iota((TOK, TOK), 0), iota((TOK, TOK), 1)
+    chosen = t_id == (r_id % SUB) * STEP + r_id // SUB
+    marks = jnp.where(chosen & (bd[...] == 1), 1.0, 0.0).astype(BF16)
+    keep = jnp.where(dot(marks, jnp.ones((TOK, 128), BF16), NN) > 0.5, F32(0.6), F32(1.0))
+    for h in range(2):
+        for part in range(2):
+            kl[2 * h + part] = keep * lam[h][part][0:1]
+
     pl.semaphore_wait(barrier, len(partners))
     for d in range(1, n_x):
         pl.semaphore_signal(ready, inc=1, device_id=at_x(d), device_id_type=MESH)
@@ -130,32 +156,6 @@
         )
         a2a[-1].start()
 
-    for copy in small:
-        copy.wait()
-    pick = (iota((32, 128), 1) % 32 == iota((32, 128), 0)).astype(F32)
-    acode = fdot(ac[...].astype(F32), pick, NN)
-    rcode = fdot(rc[...].astype(F32), pick, NN)
-    radius = 1.0 - jnp.exp2(-(4.0 + rcode * (10.0 / 1024.0)))
-    angle = acode * (math.pi / 4096.0)
-    lam_r, lam_i = radius * jnp.cos(angle), -radius * jnp.sin(angle)
-    lam = []
-    for h in range(2):
-        mine = iota((NB, 128), 0) == 4 * h + iota((NB, 128), 1) // 32
-        lam.append(
-            tuple(
-                jnp.broadcast_to(jnp.sum(jnp.where(mine, v, 0.0), axis=0, keepdims=True), (SUB, 128))
-                for v in (lam_r, lam_i)
-            )
-        )
-
-    r_id, t_id = iota((TOK, TOK), 0), iota((TOK, TOK), 1)
-    chosen = t_id == (r_id % SUB) * STEP + r_id // SUB
-    marks = jnp.where(chosen & (bd[...] == 1), 1.0, 0.0).astype(BF16)
-    keep = jnp.where(dot(marks, jnp.ones((TOK, 128), BF16), NN) > 0.5, F32(0.6), F32(1.0))
-    for h in range(2):
-        for part in range(2):
-            kl[2 * h + part] = keep * lam[h][part][0:1]
-
     lane = iota((BS, 256), 1)
     spread = (iota((NB, 256), 1) // 32 == iota((NB, 256), 0)).astype(F32)
     xs = [(iota((BS, 256), 0) == 2 * (lane % 32) + part).astype(F32) for part in range(2)]
@@ -201,8 +201,11 @@
     def later(v, m):
         return tuple(pltpu.roll(p, SUB - m, 0) for p in v)
 
+    def earlier(v, m):
+        return tuple(pltpu.roll(p, m, 0) for p in v)
+
     zero = (jnp.zeros((SUB, 128), F32), jnp.zeros((SUB, 128), F32))
-    hops, base = [], []
+    hops, base, head = [], [], []
     for h in range(2):
         steps = [cwhere(sub < SUB - 1, m1[h], zero)]
         b = cwhere(sub < SUB - 1, later(m1[h], 1), one)
@@ -210,8 +213,12 @@
             if m > 1:
                 steps.append(cmul(steps[-1], later(steps[-1], m // 2)))
             b = cmul(b, cwhere(sub < SUB - m, later(b, m), one))
+        a = cwhere(sub >= 1, earlier(m1[h], 1), one)
+        for m in (1, 2, 4):
+            a = cmul(a, cwhere(sub >= m, earlier(a, m), one))
         hops.append(steps)
         base.append(b)
+        head.append(a)
 
     def enter(i, _):
         for u in range(4):
@@ -220,6 +227,15 @@
         return 0
 
     lax.fori_loop(0, STEP // 4, enter, 0)
+
+    def leave(i, w):
+        for u in range(4):
+            q = 4 * i + u
+            put_t(fw, q, w)
+            w = [cmul(a, b) for a, b in zip(at_q(kl, q), w)]
+        return w
+
+    lax.fori_loop(0, STEP // 4, leave, head)
     mu = [(un[2 * h, 0:1, :], un[2 * h + 1, 0:1, :]) for h in range(2)]
 
     def with_prev(ref, h):
@@ -230,7 +246,7 @@
     def half(k):
         return pl.ds(pl.multiple_of(k * 256, 256), 256)
 
-    n_own = n_x // 2
+    n_own = n_x
     deep = BS // n_own
 
     def slab(k):
@@ -250,31 +266,27 @@
         qc[:, 256 * h : 256 * h + 256] = with_prev(un, h)
     to_q = scatter_x(qc, rq, qss, qsr)
 
+    def piece(k, total):
+        at = pl.ds(pl.multiple_of(k * rows, rows), rows)
+        out = []
+        for h in range(2):
+            part = g[at, 256 * h : 256 * h + 256]
+            turned = dot(part, whi[h], NN) + dot(part, wlo[h], NN)
+            c = turned[:, :128], turned[:, 128:]
+            cn[2 * h, at, :], cn[2 * h + 1, at, :] = c
+            term = cmul((fw[2 * h, at, :], fw[2 * h + 1, at, :]), c)
+            out.append(cadd(total[h], tuple(jnp.sum(v.reshape(rows // 8, 8, 128), axis=0) for v in term)))
+        return out
+
     load_own.wait()
-    for copy in a2a:
-        copy.wait_recv()
-    for h in range(2):
-        rows_h = g[:, 256 * h : 256 * h + 256]
-        turned = dot(rows_h, whi[h], NN) + dot(rows_h, wlo[h], NN)
-        cn[2 * h] = turned[:, :128]
-        cn[2 * h + 1] = turned[:, 128:]
-
-    def back(i, c):
-        for u in range(4):
-            q = STEP - 1 - (4 * i + u)
-            c = [cadd(a, cmul(b, v)) for a, b, v in zip(at_t(cn, q), at_q(kl, q), c)]
-            put_t(cn, q, c)
-        return c
-
-    first = lax.fori_loop(0, STEP // 4, back, [zero, zero])
-    entering, me = [], x * n_zl + zl
-    for h in range(2):
-        v = first[h]
-        for m, step in zip((1, 2, 4), hops[h]):
-            v = cadd(v, cmul(step, later(v, m)))
-        entering.append(cwhere(sub < SUB - 1, later(v, 1), zero))
+    carry = piece(y, [zero, zero])
+    for d in reversed(far_first(n_y)):
+        a2a[d - 1].wait_recv()
+        carry = piece(lax.rem(y + n_y - d, n_y), carry)
+    me = x * n_zl + zl
+    for h in range(2):
         for part in range(2):
-            bc[me, 2 * part + h : 2 * part + h + 1, :] = v[part][0:1]
+            bc[me, 2 * part + h : 2 * part + h + 1, :] = jnp.sum(carry[h][part], axis=0, keepdims=True)
             bc[me, 4 + 2 * part + h : 5 + 2 * part + h, :] = mu[h][part]
 
     pl.semaphore_wait(ready, n_x - 1)
@@ -285,6 +297,21 @@
     ]
     for copy in carries:
         copy.start()
+
+    def back(i, c):
+        for u in range(4):
+            q = STEP - 1 - (4 * i + u)
+            c = [cadd(a, cmul(b, v)) for a, b, v in zip(at_t(cn, q), at_q(kl, q), c)]
+            put_t(cn, q, c)
+        return c
+
+    first = lax.fori_loop(0, STEP // 4, back, [zero, zero])
+    entering = []
+    for h in range(2):
+        v = first[h]
+        for m, step in zip((1, 2, 4), hops[h]):
+            v = cadd(v, cmul(step, later(v, m)))
+        entering.append(cwhere(sub < SUB - 1, later(v, 1), zero))
 
     def fix(i, _):
         for u in range(4):
@@ -377,14 +404,22 @@
         copy.wait_send()
 
 
+def store(gi, gt, gi_out, gt_out, sem):
+    copies = [pltpu.make_async_copy(gi, gi_out, sem.at[0]), pltpu.make_async_copy(gt, gt_out, sem.at[1])]
+    for copy in copies:
+        copy.start()
+    for copy in copies:
+        copy.wait()
+
+
 def body(sizes, *operands):
     n_zh, n_core, n_x, n_zl, n_y = sizes
     n_z = n_zh * n_zl
-    slab = BS // (n_x // 2)
+    slab = BS // n_x
     vmem, anywhere = pl.BlockSpec(memory_space=pltpu.VMEM), pl.BlockSpec(memory_space=pltpu.HBM)
     plane = pltpu.VMEM((4, TOK, 128), F32)
     dma = pltpu.SemaphoreType.DMA
-    return pl.pallas_call(
+    made = pl.pallas_call(
         functools.partial(kernel, sizes),
         out_shape=(
             jax.ShapeDtypeStruct((1, TOK, CH), BF16),
@@ -401,7 +436,7 @@
             pltpu.VMEM((TOK, CH), BF16),
             pltpu.VMEM((2, 256, 256), BF16),
             pltpu.VMEM((2, 256, 256), BF16),
-            plane, plane, plane, plane,
+            plane, plane, plane, plane, plane,
             pltpu.VMEM((BS, CH), F32),
             pltpu.VMEM((n_x, slab, CH), F32),
             pltpu.VMEM((BS, CH), F32),
@@ -427,6 +462,14 @@
             collective_id=0, has_side_effects=True, vmem_limit_bytes=32 * 2**20
         ),
     )(*(pltpu.with_memory_space_constraint(a, pltpu.HBM) for a in operands))
+    return pl.pallas_call(
+        store,
+        out_shape=tuple(jax.ShapeDtypeStruct(a.shape, a.dtype) for a in made),
+        in_specs=[vmem] * 2,
+        out_specs=(anywhere, anywhere),
+        scratch_shapes=[dma((2,))],
+        compiler_params=pltpu.CompilerParams(vmem_limit_bytes=16 * 2**20),
+    )(*made)
 
 
 def solution(mesh):

time: 56 us -> 54.3 us (0.970)
  local copies, waits for them, and re-layouts: 1.41 us -> 0 us
    unnamed x2 -> x0, local copies, waits for them, and re-layouts: 1.41 us -> none
    pallas_call x1, Pallas kernels: 53.8 us -> 52.7 us  [body(): pl.pallas_call(functools.partial(kernel, sizes), out_shape=(jax.ShapeDtyp...]
    pallas_call x0 -> x1, Pallas kernels: none -> 0.81 us  [body(): pl.pallas_call(store, out_shape=tuple((jax.ShapeDtypeStruct(a.shape, a.dt...]
where the time goes in v4:
time: 54.3 us; the launch traced here: 54.2 us
  Pallas kernels  53.5 us (99%)
  between operations  0.64 us (1%)
    pallas_call x1, Pallas kernels, body(): pl.pallas_call(functools.partial(kernel, sizes), out_shape=(jax.ShapeDtyp...  52.7 us

profile of v4, /device:TPU:1, one launch (start us, length us, event | category | flops | bytes accessed | tf_op | source)
XLA Modules:
  0.0 54.2 jit_solution(9149820491412424699)
XLA Ops:
  0.6 52.7 %shard_map.77 = (bf16[1,256,512]{2,1,0:T(8,128)(2,1)S(1)}, f32[8,64,64]{2,1,0:T(8,128)S(1)}) custom-call(bf16[1,32,4096]{2,1,0:T(8,128)(2,1)} %og.1, bf16[1,256,512]{2,1,0:T(8,128)(2,1)} %ps.1, s32[1,256]{1,0:T(1,128)} %bd_in.1, s32[8,32]{1,0:T(8,128)} %ac_in.1, s32[8,32]{1,0:T(8,128)} %rc_in.1, f32[8,4,64]{2,1,0:T(4,128)} %rf_in.1), custom_call_target="tpu_custom_call" | custom-call | tf_op jit(solution)/shard_map/pallas_call | solution.py:422
  53.4 0.8 %shard_map.78 = (bf16[1,256,512]{2,1,0:T(8,128)(2,1)}, f32[8,64,64]{2,1,0:T(8,128)}) custom-call(bf16[1,256,512]{2,1,0:T(8,128)(2,1)S(1)} %get-tuple-element.4.gi, f32[8,64,64]{2,1,0:T(8,128)S(1)} %get-tuple-element.5.gt), custom_call_target="tpu_custom_call" | custom-call | tf_op jit(solution)/shard_map/pallas_call | solution.py:465

commit v5 on v4

--- a/solution.py
+++ b/solution.py
@@ -64,7 +64,7 @@
 
 def kernel(
     sizes, og, ps, bd_in, ac_in, rc_in, rf_in, gi, gt,
-    bd, ac, rc, rf, g, pv, whi, wlo, kl, wq, fw, un, cn, qc, rq, gc, gr, bc, gsum, rcore, rx, eq, req, rz,
+    bd, ac, rc, rf, g, pv, whi, wlo, kl, wq, fw, un, cn, qc, rq, gc, gr, bc, ab, gsum, rcore, rx, eq, req, rz,
     lsem, ysend, yrecv, qss, qsr, bcs, bcr, css, csr, xss, xsr, zss, zsr, xas, xar, ready,
 ):
     n_zh, n_core, n_x, n_zl, n_y = sizes
@@ -201,11 +201,8 @@
     def later(v, m):
         return tuple(pltpu.roll(p, SUB - m, 0) for p in v)
 
-    def earlier(v, m):
-        return tuple(pltpu.roll(p, m, 0) for p in v)
-
     zero = (jnp.zeros((SUB, 128), F32), jnp.zeros((SUB, 128), F32))
-    hops, base, head = [], [], []
+    hops, base = [], []
     for h in range(2):
         steps = [cwhere(sub < SUB - 1, m1[h], zero)]
         b = cwhere(sub < SUB - 1, later(m1[h], 1), one)
@@ -213,12 +210,8 @@
             if m > 1:
                 steps.append(cmul(steps[-1], later(steps[-1], m // 2)))
             b = cmul(b, cwhere(sub < SUB - m, later(b, m), one))
-        a = cwhere(sub >= 1, earlier(m1[h], 1), one)
-        for m in (1, 2, 4):
-            a = cmul(a, cwhere(sub >= m, earlier(a, m), one))
         hops.append(steps)
         base.append(b)
-        head.append(a)
 
     def enter(i, _):
         for u in range(4):
@@ -235,16 +228,16 @@
             w = [cmul(a, b) for a, b in zip(at_q(kl, q), w)]
         return w
 
-    lax.fori_loop(0, STEP // 4, leave, head)
+    lax.fori_loop(0, STEP // 4, leave, [one, one])
     mu = [(un[2 * h, 0:1, :], un[2 * h + 1, 0:1, :]) for h in range(2)]
 
+    def half(k):
+        return pl.ds(pl.multiple_of(k * 256, 256), 256)
+
     def with_prev(ref, h):
-        prev = pv[:, 256 * h : 256 * h + 256]
+        prev = pv[:, half(h)]
         hi, lo = split(jnp.concatenate([ref[2 * h], ref[2 * h + 1]], axis=1))
         return compact(dot(prev, hi, TN) + dot(prev, lo, TN))
-
-    def half(k):
-        return pl.ds(pl.multiple_of(k * 256, 256), 256)
 
     n_own = n_x
     deep = BS // n_own
@@ -266,32 +259,41 @@
         qc[:, 256 * h : 256 * h + 256] = with_prev(un, h)
     to_q = scatter_x(qc, rq, qss, qsr)
 
-    def piece(k, total):
+    me = x * n_zl + zl
+    for h in range(2):
+        for part in range(2):
+            bc[me, 4 + 2 * part + h : 5 + 2 * part + h, :] = mu[h][part]
+    pl.semaphore_wait(ready, n_x - 1)
+    offsets = [(d, e) for d in range(n_x) for e in range(n_zl) if d or e]
+    offsets.sort(key=lambda o: -min(o[0], n_x - o[0]) - min(o[1], n_zl - o[1]))
+
+    subs = rows // STEP
+
+    def piece(k):
         at = pl.ds(pl.multiple_of(k * rows, rows), rows)
-        out = []
         for h in range(2):
             part = g[at, 256 * h : 256 * h + 256]
             turned = dot(part, whi[h], NN) + dot(part, wlo[h], NN)
             c = turned[:, :128], turned[:, 128:]
             cn[2 * h, at, :], cn[2 * h + 1, at, :] = c
             term = cmul((fw[2 * h, at, :], fw[2 * h + 1, at, :]), c)
-            out.append(cadd(total[h], tuple(jnp.sum(v.reshape(rows // 8, 8, 128), axis=0) for v in term)))
-        return out
+            for i in range(2):
+                ab[2 * h + i, pl.ds(k * subs, subs), :] = jnp.sum(term[i].reshape(subs, STEP, 128), axis=1)
 
     load_own.wait()
-    carry = piece(y, [zero, zero])
+    piece(y)
     for d in reversed(far_first(n_y)):
         a2a[d - 1].wait_recv()
-        carry = piece(lax.rem(y + n_y - d, n_y), carry)
-    me = x * n_zl + zl
-    for h in range(2):
+        piece(lax.rem(y + n_y - d, n_y))
+    entering = []
+    for h in range(2):
+        v = (ab[2 * h], ab[2 * h + 1])
+        for m, step in zip((1, 2, 4), hops[h]):
+            v = cadd(v, cmul(step, later(v, m)))
+        entering.append(cwhere(sub < SUB - 1, later(v, 1), zero))
         for part in range(2):
-            bc[me, 2 * part + h : 2 * part + h + 1, :] = jnp.sum(carry[h][part], axis=0, keepdims=True)
-            bc[me, 4 + 2 * part + h : 5 + 2 * part + h, :] = mu[h][part]
-
-    pl.semaphore_wait(ready, n_x - 1)
-    offsets = [(d, e) for d in range(n_x) for e in range(n_zl) if d or e]
-    offsets.sort(key=lambda o: -min(o[0], n_x - o[0]) - min(o[1], n_zl - o[1]))
+            bc[me, 2 * part + h : 2 * part + h + 1, :] = v[part][0:1]
+
     carries = [
         remote(bc.at[me], bc.at[me], bcs.at[i], bcr.at[i], at_ctx(*o)) for i, o in enumerate(offsets)
     ]
@@ -305,25 +307,11 @@
             put_t(cn, q, c)
         return c
 
-    first = lax.fori_loop(0, STEP // 4, back, [zero, zero])
-    entering = []
-    for h in range(2):
-        v = first[h]
-        for m, step in zip((1, 2, 4), hops[h]):
-            v = cadd(v, cmul(step, later(v, m)))
-        entering.append(cwhere(sub < SUB - 1, later(v, 1), zero))
-
-    def fix(i, _):
-        for u in range(4):
-            q = 4 * i + u
-            put_t(cn, q, [cadd(a, cmul(b, v)) for a, b, v in zip(at_t(cn, q), at_q(wq, q), entering)])
-        return 0
-
-    lax.fori_loop(0, STEP // 4, fix, 0)
-    for h in range(2):
-        gc[:, 256 * h : 256 * h + 256] = with_prev(cn, h)
+    lax.fori_loop(0, STEP // 4, back, entering)
+    gc[:, half(1 - core)] = with_prev(cn, 1 - core)
     to_core = remote(gc.at[:, half(1 - core)], rcore, css.at[0], csr.at[0], sibling)
     to_core.start()
+    gc[:, half(core)] = with_prev(cn, core)
     to_core.wait_recv()
     gsum[...] = gc[:, half(core)] + rcore[...]
     to_x = scatter_x(gsum, rx, xss, xsr)
@@ -400,7 +388,7 @@
     back_core.wait_recv()
     finish(1 - core)
 
-    for copy in a2a + to_q + carries + [to_core] + to_x + [to_core_2] + to_z + back_x + [back_core]:
+    for copy in a2a + to_q  + carries + [to_core] + to_x + [to_core_2] + to_z + back_x + [back_core]:
         copy.wait_send()
 
 
@@ -442,6 +430,7 @@
             pltpu.VMEM((BS, CH), F32),
             pltpu.VMEM((BS, CH), F32),
             pltpu.VMEM((n_x * n_zl, 8, 128), F32),
+            pltpu.VMEM((4, SUB, 128), F32),
             pltpu.VMEM((BS, 256), F32),
             pltpu.VMEM((BS, 256), F32),
             pltpu.VMEM((n_x, slab, 256), F32),

time: 54.3 us -> 54.4 us (level)
  no operation moved by 1% of the time
where the time goes in v5:
time: 54.4 us; the launch traced here: 54.2 us
  Pallas kernels  53.6 us (99%)
  between operations  0.64 us (1%)
    pallas_call x1, Pallas kernels, body(): pl.pallas_call(functools.partial(kernel, sizes), out_shape=(jax.ShapeDtyp...  52.8 us

profile of v5, /device:TPU:1, one launch (start us, length us, event | category | flops | bytes accessed | tf_op | source)
XLA Modules:
  0.0 54.2 jit_solution(3053228286907270221)
XLA Ops:
  0.6 52.8 %shard_map.77 = (bf16[1,256,512]{2,1,0:T(8,128)(2,1)S(1)}, f32[8,64,64]{2,1,0:T(8,128)S(1)}) custom-call(bf16[1,32,4096]{2,1,0:T(8,128)(2,1)} %og.1, bf16[1,256,512]{2,1,0:T(8,128)(2,1)} %ps.1, s32[1,256]{1,0:T(1,128)} %bd_in.1, s32[8,32]{1,0:T(8,128)} %ac_in.1, s32[8,32]{1,0:T(8,128)} %rc_in.1, f32[8,4,64]{2,1,0:T(4,128)} %rf_in.1), custom_call_target="tpu_custom_call" | custom-call | tf_op jit(solution)/shard_map/pallas_call | solution.py:410
  53.4 0.8 %shard_map.78 = (bf16[1,256,512]{2,1,0:T(8,128)(2,1)}, f32[8,64,64]{2,1,0:T(8,128)}) custom-call(bf16[1,256,512]{2,1,0:T(8,128)(2,1)S(1)} %get-tuple-element.4.gi, f32[8,64,64]{2,1,0:T(8,128)S(1)} %get-tuple-element.5.gt), custom_call_target="tpu_custom_call" | custom-call | tf_op jit(solution)/shard_map/pallas_call | solution.py:454

commit v6 on v5

--- a/solution.py
+++ b/solution.py
@@ -375,20 +375,23 @@
         where = at_x(d if d <= n_own // 2 else n_x - n_own + d)
         back_x.append(remote(mine, mine, xas.at[i], xar.at[i], where))
         back_x[-1].start()
-    for copy in back_x:
-        copy.wait_recv()
-    ours = gr.at[:, half(core)]
-    back_core = remote(ours, ours, css.at[2], csr.at[2], sibling)
-    back_core.start()
+    back_core = [remote(mine, mine, css.at[2], csr.at[2], sibling)]
+    back_core[0].start()
+    for i, d in reversed(list(enumerate(far_first(n_own)))):
+        back_x[i].wait_recv()
+        part = gr.at[slab(lax.rem(x + n_x - d, n_x)), half(core)]
+        back_core.append(remote(part, part, css.at[3 + i], csr.at[3 + i], sibling))
+        back_core[-1].start()
 
     def finish(h):
         gt[pl.ds(4 * h, 4)] = gr[:, half(h)].T.reshape(4, BS, BS)
 
     finish(core)
-    back_core.wait_recv()
+    for copy in back_core:
+        copy.wait_recv()
     finish(1 - core)
 
-    for copy in a2a + to_q  + carries + [to_core] + to_x + [to_core_2] + to_z + back_x + [back_core]:
+    for copy in a2a + to_q  + carries + [to_core] + to_x + [to_core_2] + to_z + back_x + back_core:
         copy.wait_send()
 
 
@@ -441,7 +444,7 @@
             dma((n_y,)), dma((n_y,)),
             dma((n_x,)), dma((n_x,)),
             dma((n_x * n_zl,)), dma((n_x * n_zl,)),
-            dma((3,)), dma((3,)),
+            dma((3 + n_x,)), dma((3 + n_x,)),
             dma((n_x,)), dma((n_x,)),
             dma((n_z,)), dma((n_z,)),
             dma((n_x,)), dma((n_x,)),

time: 54.4 us -> 54.5 us (level)
  no operation moved by 1% of the time
where the time goes in v6:
time: 54.5 us; the launch traced here: 54.3 us
  Pallas kernels  53.7 us (99%)
  between operations  0.64 us (1%)
    pallas_call x1, Pallas kernels, body(): pl.pallas_call(functools.partial(kernel, sizes), out_shape=(jax.ShapeDtyp...  52.9 us

profile of v6, /device:TPU:1, one launch (start us, length us, event | category | flops | bytes accessed | tf_op | source)
XLA Modules:
  0.0 54.3 jit_solution(17613902032623356045)
XLA Ops:
  0.6 52.9 %shard_map.77 = (bf16[1,256,512]{2,1,0:T(8,128)(2,1)S(1)}, f32[8,64,64]{2,1,0:T(8,128)S(1)}) custom-call(bf16[1,32,4096]{2,1,0:T(8,128)(2,1)} %og.1, bf16[1,256,512]{2,1,0:T(8,128)(2,1)} %ps.1, s32[1,256]{1,0:T(1,128)} %bd_in.1, s32[8,32]{1,0:T(8,128)} %ac_in.1, s32[8,32]{1,0:T(8,128)} %rc_in.1, f32[8,4,64]{2,1,0:T(4,128)} %rf_in.1), custom_call_target="tpu_custom_call" | custom-call | tf_op jit(solution)/shard_map/pallas_call | solution.py:413
  53.5 0.8 %shard_map.78 = (bf16[1,256,512]{2,1,0:T(8,128)(2,1)}, f32[8,64,64]{2,1,0:T(8,128)}) custom-call(bf16[1,256,512]{2,1,0:T(8,128)(2,1)S(1)} %get-tuple-element.4.gi, f32[8,64,64]{2,1,0:T(8,128)S(1)} %get-tuple-element.5.gt), custom_call_target="tpu_custom_call" | custom-call | tf_op jit(solution)/shard_map/pallas_call | solution.py:457
